TPU v7x, 512 devices: a whole 4x8x8 slice. The times are simulated.
512 devices in a mesh: gx: 8 (over z), yz: 64 (over x, y, core).
Axes of the slice: x: 4, y: 8, z: 8, core: 2. Of those that a mesh axis runs over, the one named last changes fastest.
Arguments:
- system_source_term: float32 [320, 65536], P(None, ('gx', 'yz')), may hold values from -200 to 200
- mass_plus_source: float32 [320, 65536], P(None, ('gx', 'yz')), may hold values from 1 to 4
- lifted_upwind_coupling: float32 [480, 65536], P(None, ('gx', 'yz')), may hold values from 0.5 to 2
- frozen_direction_derivative: float32 [75, 65536], P(None, ('gx', 'yz')), may hold values from -3 to 3
- first_solve_matrix: float32 [320, 320], replicated, may hold values from -0.3125 to 0.3125
- final_solve_matrix: float32 [320, 320], replicated, may hold values from -0.3125 to 0.3125
- middle_cell_matrices: float32 [320, 65536], P(None, ('gx', 'yz')), may hold values from 0.3 to 3
- adjacent_table_slots: int32 [6, 65536], P(None, ('gx', 'yz')), may hold values from 0 to 1296, as said below
- plane_outgoing_cells: int32 [512, 2, 16], P(('gx', 'yz')), may hold values from 0 to 127
- band_outgoing_cells: int32 [512, 2, 16], P(('gx', 'yz')), may hold values from 0 to 127
- small_side_table_slot: int32 [512, 384], P(('gx', 'yz')), may hold values from 0 to 768, as said below
- proprietor_mortar_index: int32 [512, 384], P(('gx', 'yz')), may hold values from 0 to 80, as said below
- outgoing_quadrant_index: int32 [512, 384], P(('gx', 'yz')), may hold values from 0 to 3, as said below
- incoming_mortar_index: int32 [512, 384], P(('gx', 'yz')), may hold values from 0 to 80
- incoming_quadrant_index: int32 [512, 384], P(('gx', 'yz')), may hold values from 0 to 3, as said below
- coarse_mortar_table_slot: int32 [512, 80], P(('gx', 'yz')), may hold values from 0 to 767
Outputs:
- newton_update: float32 [320, 65536], P(None, ('gx', 'yz'))
Inputs may be any that keep to these rules, and one draw needn't show every extreme that they name: `adjacent_table_slots`: column of the neighbour trace in the device's table; 1296 marks a boundary face. `small_side_table_slot`: 768 marks an empty slot, exactly where proprietor_mortar_index is 80. Send slot (m, c) of device (g, k) and receive slot (k, c) of device (g, m) hold the same tile: there proprietor_mortar_index, outgoing_quadrant_index equal incoming_mortar_index, incoming_quadrant_index here; 80 marks an empty slot; no position of an owner's hanging face is sent twice; the live hanging faces of an owner are its first ones; from one device to one owner go at most 6 tiles, a bound reached in every draw; in each gx plane one owner receives 4 * 80 tiles. `outgoing_quadrant_index`: 0 in empty slots. `incoming_quadrant_index`: 0 in empty slots.
All inputs are finite; a program needn't handle non-finite values.
Results may differ from a plain program's by a relative error of at most 0.0003.
Values sent between devices are 32-bit elements; how exact they have to be, the bound alone decides.
A program may use at most 64 MiB of HBM per device.

v0:
```python
import jax
import jax.numpy as jnp
import numpy as np
from jax import lax
from jax.sharding import PartitionSpec as P

ITERS = 2


maximum_depth = lax.Precision.HIGHEST
epsilon = 1e-06


def with_halo(shard, sides, width, wrap):
    for axis, dim in sides:
        size, length = (lax.axis_size(axis), shard.shape[dim])
        up = [(i, (i + 1) % size) for i in range(size if wrap else size - 1)]
        down = [(j, i) for i, j in up]
        last = lax.slice_in_dim(shard, length - width, length, axis=dim)
        leading = lax.slice_in_dim(shard, 0, width, axis=dim)
        before = lax.ppermute(last, axis, up)
        after = lax.ppermute(leading, axis, down)
        shard = jnp.concatenate([before, shard, after], axis=dim)
    return shard


def gll_tables():
    inv_root = 1.0 / np.sqrt(5.0)
    gll_points = np.array([-1.0, -inv_root, inv_root, 1.0])
    weights = np.array([1.0, 5.0, 5.0, 1.0]) / 6.0

    def lagrange(points):
        values_at = np.ones((len(points), 4))
        for table_slot_index in range(4):
            for m in range(4):
                if m != table_slot_index:
                    values_at[:, table_slot_index] = (
                        values_at[:, table_slot_index]
                        * (points - gll_points[m])
                        / (gll_points[table_slot_index] - gll_points[m])
                    )
        return values_at

    derivative = np.zeros((4, 4))
    for i in range(4):
        for table_slot_index in range(4):
            summed = 0.0
            for m in range(4):
                if m != table_slot_index:
                    product_term = 1.0 / (gll_points[table_slot_index] - gll_points[m])
                    for n in range(4):
                        if n != table_slot_index and n != m:
                            product_term = (
                                product_term
                                * (gll_points[i] - gll_points[n])
                                / (gll_points[table_slot_index] - gll_points[n])
                            )
                    summed = summed + product_term
            derivative[i, table_slot_index] = summed
    halves = [lagrange((gll_points - 1.0) / 2.0), lagrange((gll_points + 1.0) / 2.0)]
    half_projections = [
        0.5 * (1.0 / weights)[:, None] * halve.T * weights[None, :] for halve in halves
    ]
    interpolate = np.stack([np.kron(halves[q // 2], halves[q % 2]) for q in range(4)])
    projection = np.stack(
        [np.kron(half_projections[q // 2], half_projections[q % 2]) for q in range(4)]
    )
    identity_four = np.eye(4)
    node_derivative = np.stack(
        [
            np.kron(derivative, np.kron(identity_four, identity_four)),
            np.kron(identity_four, np.kron(derivative, identity_four)),
            np.kron(identity_four, np.kron(identity_four, derivative)),
        ]
    )
    selection = np.zeros((6, 16, 64))
    for face_id in range(6):
        direction = face_id // 2
        fixed_node = 0 if face_id % 2 == 0 else 3
        for first in range(4):
            for second in range(4):
                if direction == 0:
                    node = fixed_node * 16 + first * 4 + second
                elif direction == 1:
                    node = first * 16 + fixed_node * 4 + second
                else:
                    node = first * 16 + second * 4 + fixed_node
                selection[face_id, first * 4 + second, node] = 1.0
    lifting = selection.transpose(2, 0, 1)
    return (
        jnp.asarray(node_derivative, jnp.float32),
        jnp.asarray(interpolate, jnp.float32),
        jnp.asarray(projection, jnp.float32),
        jnp.asarray(selection, jnp.float32),
        jnp.asarray(lifting, jnp.float32),
    )


def own_traces(argument_array, selection):
    local_count = argument_array.shape[1]
    nodal_view = argument_array.reshape(5, 64, local_count)
    faces = jnp.einsum("fsn,ane->asfe", selection, nodal_view, precision=maximum_depth)
    return faces.reshape(80, 6 * local_count)


def jacobian(
    argument_array,
    own_faces,
    near_faces,
    mass_plus_source,
    lifted_upwind_coupling,
    frozen_direction_derivative,
    node_derivative,
    lifting,
):
    local_count = argument_array.shape[1]
    nodal_view = argument_array.reshape(5, 64, local_count)
    flux_blocks = frozen_direction_derivative.reshape(3, 5, 5, local_count)
    flux_terms = jnp.einsum("dabe,bne->dane", flux_blocks, nodal_view, precision=maximum_depth)
    derived = jnp.einsum("dmn,dane->ame", node_derivative, flux_terms, precision=maximum_depth)
    difference = (own_faces - near_faces).reshape(5, 16, 6, local_count)
    coupling = lifted_upwind_coupling.reshape(6, 5, 16, local_count)
    lifted = jnp.einsum(
        "nfs,fase,asfe->ane", lifting, coupling, difference, precision=maximum_depth
    )
    return mass_plus_source * argument_array + (derived + lifted).reshape(320, local_count)


def solve_cell_system(argument_array, first_solve_matrix, final_solve_matrix, middle_cell_matrices):
    interior_share = jnp.dot(
        first_solve_matrix,
        argument_array,
        precision=maximum_depth,
        preferred_element_type=jnp.float32,
    )
    return jnp.dot(
        final_solve_matrix,
        middle_cell_matrices * interior_share,
        precision=maximum_depth,
        preferred_element_type=jnp.float32,
    )


def mortar_sums(received, incoming_mortar_index, incoming_quadrant_index, projection, hang_count):
    slot_count = received.shape[1]
    face_values = received.reshape(5, 16, slot_count)
    candidates = jnp.einsum("qmn,anc->qamc", projection, face_values, precision=maximum_depth)
    selector_q = (
        incoming_quadrant_index[None, :] == jnp.arange(4, dtype=jnp.int32)[:, None]
    ).astype(jnp.float32)
    projected = jnp.sum(candidates * selector_q[:, None, None, :], axis=0).reshape(80, slot_count)
    onehot = (
        incoming_mortar_index[:, None] == jnp.arange(hang_count, dtype=jnp.int32)[None, :]
    ).astype(jnp.float32)
    return jnp.dot(projected, onehot, precision=maximum_depth, preferred_element_type=jnp.float32)


def fine_replies(coarse_cols, outgoing_quadrant_index, interpolate):
    slot_count = coarse_cols.shape[1]
    face_values = coarse_cols.reshape(5, 16, slot_count)
    candidates = jnp.einsum("qmn,anc->qamc", interpolate, face_values, precision=maximum_depth)
    selector_q = (
        outgoing_quadrant_index[None, :] == jnp.arange(4, dtype=jnp.int32)[:, None]
    ).astype(jnp.float32)
    return jnp.sum(candidates * selector_q[:, None, None, :], axis=0).reshape(80, slot_count)


def least_squares(beta_norm, columns):
    steps_count = len(columns)
    zero_value = jnp.zeros((), jnp.float32)
    target = [beta_norm] + [zero_value] * steps_count
    rotations = []
    upper_rows = []
    for table_slot_index in range(steps_count):
        column = list(columns[table_slot_index])
        for i in range(len(rotations)):
            cos_value, sine_value = rotations[i]
            first_new = cos_value * column[i] + sine_value * column[i + 1]
            second = cos_value * column[i + 1] - sine_value * column[i]
            column[i] = first_new
            column[i + 1] = second
        radius = jnp.sqrt(
            column[table_slot_index] * column[table_slot_index]
            + column[table_slot_index + 1] * column[table_slot_index + 1]
        )
        cos_value = column[table_slot_index] / radius
        sine_value = column[table_slot_index + 1] / radius
        column[table_slot_index] = radius
        rotations.append((cos_value, sine_value))
        target[table_slot_index + 1] = -sine_value * target[table_slot_index]
        target[table_slot_index] = cos_value * target[table_slot_index]
        upper_rows.append(column[: table_slot_index + 1])
    coeffs = [zero_value] * steps_count
    for table_slot_index in reversed(range(steps_count)):
        running = target[table_slot_index]
        for k in range(table_slot_index + 1, steps_count):
            running = running - upper_rows[k][table_slot_index] * coeffs[k]
        coeffs[table_slot_index] = running / upper_rows[table_slot_index][table_slot_index]
    return coeffs


def inner_global(partial_value):
    return lax.psum(partial_value, ("gx", "yz"))


def on_device(
    system_source_term,
    mass_plus_source,
    lifted_upwind_coupling,
    frozen_direction_derivative,
    first_solve_matrix,
    final_solve_matrix,
    middle_cell_matrices,
    adjacent_table_slots,
    plane_outgoing_cells,
    band_outgoing_cells,
    small_side_table_slot,
    proprietor_mortar_index,
    outgoing_quadrant_index,
    incoming_mortar_index,
    incoming_quadrant_index,
    coarse_mortar_table_slot,
):
    node_derivative, interpolate, projection, selection, lifting = gll_tables()
    local_count = system_source_term.shape[1]
    hang_count = coarse_mortar_table_slot.shape[1]
    halo_width = plane_outgoing_cells.shape[2]
    near_index = adjacent_table_slots.reshape(-1)
    defect_array = solve_cell_system(
        system_source_term, first_solve_matrix, final_solve_matrix, middle_cell_matrices
    )
    beta_norm = jnp.sqrt(inner_global(jnp.sum(defect_array * defect_array)) + epsilon)
    arnoldi_directions = [defect_array / beta_norm]
    columns = []
    for table_slot_index in range(ITERS):
        argument_array = arnoldi_directions[table_slot_index]
        own_faces = own_traces(argument_array, selection)
        slab_buffer = jnp.stack(
            [
                jnp.take(own_faces, plane_outgoing_cells[0, 0], axis=1),
                jnp.take(own_faces, local_count + plane_outgoing_cells[0, 1], axis=1),
            ]
        ).reshape(2, 80 * halo_width)
        slab_padded = with_halo(slab_buffer, (("gx", 0),), 1, False)
        side_buffer = jnp.stack(
            [
                jnp.take(own_faces, 2 * local_count + band_outgoing_cells[0, 0], axis=1),
                jnp.take(own_faces, 3 * local_count + band_outgoing_cells[0, 1], axis=1),
            ]
        ).reshape(2, 80 * halo_width)
        side_padded = with_halo(side_buffer, (("yz", 0),), 1, True)
        fine_send = jnp.take(
            own_faces, small_side_table_slot[0], axis=1, mode="fill", fill_value=0.0
        )
        coarse = jnp.take(own_faces, coarse_mortar_table_slot[0], axis=1)
        outgoing = jnp.take(coarse, incoming_mortar_index[0], axis=1, mode="fill", fill_value=0.0)
        fine_recv = lax.all_to_all(fine_send, "yz", split_axis=1, concat_axis=1, tiled=True)
        coarse_cols = lax.all_to_all(outgoing, "yz", split_axis=1, concat_axis=1, tiled=True)
        hang_sum = mortar_sums(
            fine_recv, incoming_mortar_index[0], incoming_quadrant_index[0], projection, hang_count
        )
        replies = fine_replies(coarse_cols, outgoing_quadrant_index[0], interpolate)
        trace_table = jnp.concatenate(
            [
                own_faces,
                slab_padded[0].reshape(80, halo_width),
                slab_padded[3].reshape(80, halo_width),
                side_padded[0].reshape(80, halo_width),
                side_padded[3].reshape(80, halo_width),
                hang_sum,
                replies,
            ],
            axis=1,
        )
        near_faces = jnp.take(trace_table, near_index, axis=1, mode="fill", fill_value=0.0)
        scratch_storage = solve_cell_system(
            jacobian(
                argument_array,
                own_faces,
                near_faces,
                mass_plus_source,
                lifted_upwind_coupling,
                frozen_direction_derivative,
                node_derivative,
                lifting,
            ),
            first_solve_matrix,
            final_solve_matrix,
            middle_cell_matrices,
        )
        column = []
        for i in range(table_slot_index + 1):
            coefficient = inner_global(jnp.sum(scratch_storage * arnoldi_directions[i]))
            scratch_storage = scratch_storage - coefficient * arnoldi_directions[i]
            column.append(coefficient)
        new_norm = jnp.sqrt(inner_global(jnp.sum(scratch_storage * scratch_storage)) + epsilon)
        column.append(new_norm)
        columns.append(column)
        arnoldi_directions.append(scratch_storage / new_norm)
    coeffs = least_squares(beta_norm, columns)
    newton_update = coeffs[0] * arnoldi_directions[0]
    table_slot_index = 1
    newton_update = newton_update + coeffs[table_slot_index] * arnoldi_directions[table_slot_index]
    return newton_update


def solution(mesh):
    return jax.shard_map(
        on_device,
        mesh=mesh,
        in_specs=(
            P(None, ("gx", "yz")),
            P(None, ("gx", "yz")),
            P(None, ("gx", "yz")),
            P(None, ("gx", "yz")),
            P(),
            P(),
            P(None, ("gx", "yz")),
            P(None, ("gx", "yz")),
            P(("gx", "yz"), None, None),
            P(("gx", "yz"), None, None),
            P(("gx", "yz"), None),
            P(("gx", "yz"), None),
            P(("gx", "yz"), None),
            P(("gx", "yz"), None),
            P(("gx", "yz"), None),
            P(("gx", "yz"), None),
        ),
        out_specs=P(None, ("gx", "yz")),
        check_vma=False,
    )
```

profile of v0, /device:TPU:1, one launch (start us, length us, event | category | flops | bytes accessed | tf_op | source)
XLA Modules:
  0.0 749.5 jit_solution(8252775757002441700)
XLA Ops:
  0.0 1.7 convolution_multiply_fusion
  1.8 1.1 multiply_reduce_fusion.3
  2.9 106.1 %psum.42 = f32[]{:T(128)} all-reduce(f32[]{:T(128)} %get-tuple-element.22), channel_id=1, replica_groups=mesh['gx'=8,'yz'=64] {'gx','yz'}, use_global_device_ids=true, to_apply=%region_1.0 | all-reduce | flops 1 | bytes 8 | tf_op jit(solution)/shard_map/psum | solution.py:203
  112.0 1.8 collective-permute-start
  115.3 1.3 collective-permute-start.1
  118.1 3.1 collective-permute-start.2
  122.7 1.9 collective-permute-start.3
  124.7 1.1 gather_fusion.4
  126.0 1.0 reshape.387
  127.0 10.3 %all-to-all-start = ((f32[64,1,480]{2,1,0:T(1,128)}), f32[64,1,480]{2,1,0:T(1,128)}, u32[]{:S(2)}, u32[]{:S(2)}) async-start(f32[64,1,480]{2,1,0:T(1,128)} %reshape.387), calls=%async_computation | async-start | bytes 262144 | tf_op jit(solution)/shard_map/all_to_all | solution.py:257
  139.6 2.6 convolution_bitcast_fusion.1
  142.2 1.9 convolution_bitcast_fusion.13
  144.3 1.1 gather_fusion.6
  145.4 0.8 select_bitcast_fusion.2
  146.8 1.0 all_to_all.26
  147.8 1.0 reshape.389
  148.9 0.7 reduce.2
  149.8 10.7 %all-to-all-start.1 = ((f32[64,1,480]{2,1,0:T(1,128)}), f32[64,1,480]{2,1,0:T(1,128)S(1)}, u32[]{:S(2)}, u32[]{:S(2)}) async-start(f32[64,1,480]{2,1,0:T(1,128)} %reshape.389), calls=%async_computation.1 | async-start | bytes 262144 | tf_op jit(solution)/shard_map/all_to_all | solution.py:258
  162.9 1.8 reduce.13
  164.8 1.5 reshape.166
  166.3 4.5 all-to-all-done.1
  170.8 0.9 reduce.14
  171.8 1.5 reshape.168
  173.3 2.8 fusion.5
  176.1 0.8 copy.151
  176.9 2.8 fusion.4
  180.1 1.0 constant_dynamic-update-slice_fusion
  181.1 2.3 gather_fusion.7
  183.4 1.2 copy.152
  184.6 0.7 bitcast_subtract_fusion.1
  185.3 1.0 reshape.171
  186.5 1.3 fusion.10
  188.4 1.1 fusion.21
  189.6 96.9 %psum.43 = f32[]{:T(128)} all-reduce(f32[]{:T(128)} %get-tuple-element.24), channel_id=1, replica_groups=mesh['gx'=8,'yz'=64] {'gx','yz'}, use_global_device_ids=true, to_apply=%region_5.11 | all-reduce | flops 1 | bytes 8 | tf_op jit(solution)/shard_map/psum | solution.py:203
  286.5 1.3 multiply_reduce_fusion.2
  289.2 95.5 %psum.44 = f32[]{:T(128)} all-reduce(f32[]{:T(128)} %multiply_reduce_fusion.2), channel_id=1, replica_groups=mesh['gx'=8,'yz'=64] {'gx','yz'}, use_global_device_ids=true, to_apply=%region_7.13 | all-reduce | flops 1 | bytes 8 | tf_op jit(solution)/shard_map/psum | solution.py:203
  390.2 1.6 gather_fusion.12
  391.8 0.7 gather_fusion.13
  393.3 1.0 copy.187
  394.3 3.7 convolution_bitcast_fusion
  398.1 1.3 convolution_bitcast_fusion.10
  399.6 2.7 collective-permute-start.4
  402.5 1.3 collective-permute-start.5
  404.1 2.0 collective-permute-start.6
  406.3 2.8 collective-permute-start.7
  409.2 1.0 reshape.391
  410.2 10.0 %all-to-all-start.2 = ((f32[64,1,480]{2,1,0:T(1,128)}), f32[64,1,480]{2,1,0:T(1,128)S(1)}, u32[]{:S(2)}, u32[]{:S(2)}) async-start(f32[64,1,480]{2,1,0:T(1,128)} %reshape.391), calls=%async_computation.2 | async-start | bytes 262144 | tf_op jit(solution)/shard_map/all_to_all | solution.py:257
  420.3 1.1 gather_fusion.14
  421.6 1.0 reshape.393
  423.3 7.2 all-to-all-done.2
  430.5 5.6 all-to-all-start.3
  436.1 0.9 reduce.15
  437.5 2.7 fusion.6
  440.2 6.1 all-to-all-done.3
  446.3 1.8 reduce.16
  448.6 1.3 fusion.7
  450.1 1.3 convolution_dynamic-update-slice_fusion
  451.5 1.6 gather_fusion.15
  455.0 1.1 fusion.23
  456.2 96.3 %psum.45 = f32[]{:T(128)} all-reduce(f32[]{:T(128)} %get-tuple-element.26), channel_id=1, replica_groups=mesh['gx'=8,'yz'=64] {'gx','yz'}, use_global_device_ids=true, to_apply=%region_11.17 | all-reduce | flops 1 | bytes 8 | tf_op jit(solution)/shard_map/psum | solution.py:203
  552.4 1.3 multiply_reduce_fusion.1
  554.4 95.1 %psum.46 = f32[]{:T(128)} all-reduce(f32[]{:T(128)} %multiply_reduce_fusion.1), channel_id=1, replica_groups=mesh['gx'=8,'yz'=64] {'gx','yz'}, use_global_device_ids=true, to_apply=%region_13.19 | all-reduce | flops 1 | bytes 8 | tf_op jit(solution)/shard_map/psum | solution.py:203
  650.0 1.9 multiply_reduce_fusion
  653.1 94.6 %psum.47 = f32[]{:T(128)} all-reduce(f32[]{:T(128)} %multiply_reduce_fusion), channel_id=1, replica_groups=mesh['gx'=8,'yz'=64] {'gx','yz'}, use_global_device_ids=true, to_apply=%region_15.21 | all-reduce | flops 1 | bytes 8 | tf_op jit(solution)/shard_map/psum | solution.py:203
  (275 shorter events, 23.8 us)
Async XLA Ops:
  0.0 109.7 %copy-start.21 = (f32[6,16,64,1]{2,1,0,3:T(8,128)S(1)}, f32[6,16,64,1]{2,1,0,3:T(8,128)}, u32[]{:S(2)}) copy-start(f32[6,16,64,1]{2,1,0,3:T(8,128)} %constant.89) | copy-start | bytes 73732
  1.8 109.3 %copy-start.65 = (s32[1,2,16]{2,1,0:T(2,128)S(1)}, s32[1,2,16]{2,1,0:T(2,128)}, u32[]{:S(2)}) copy-start(s32[1,2,16]{2,1,0:T(2,128)} %param.39) | copy-start | bytes 388
  109.7 28.3 %copy-start.3 = (f32[128,320]{0,1:T(8,128)}, f32[128,320]{0,1:T(8,128)S(1)}, u32[]{:S(2)}) copy-start(f32[128,320]{0,1:T(8,128)S(1)} %broadcast_divide_fusion.1) | copy-start | bytes 491524
  109.7 6.8 copy-start.66
  110.2 14.4 %copy-start.61 = (s32[1,384]{1,0:T(1,128)S(1)}, s32[1,384]{1,0:T(1,128)}, u32[]{:S(2)}) copy-start(s32[1,384]{1,0:T(1,128)} %param.41) | copy-start | bytes 4612
  111.1 13.5 %copy-start.51 = (pred[16]{0:T(512)(128)(4,1)}, pred[16]{0:T(512)(128)(4,1)S(1)}, u32[]{:S(2)}) copy-start(pred[16]{0:T(512)(128)(4,1)S(1)} %get-tuple-element.14) | copy-start | bytes 52
  111.1 14.8 %copy-start.53 = (pred[16]{0:T(512)(128)(4,1)}, pred[16]{0:T(512)(128)(4,1)S(1)}, u32[]{:S(2)}) copy-start(pred[16]{0:T(512)(128)(4,1)S(1)} %get-tuple-element.20) | copy-start | bytes 52
  112.0 36.8 %collective-permute-start = (f32[1,1280]{1,0:T(1,128)S(1)}, f32[1,1280]{1,0:T(1,128)S(1)}, u32[]{:S(2)}, u32[]{:S(2)}) collective-permute-start(f32[1,1280]{1,0:T(1,128)S(1)} %slice.49), channel_id=1, source_target_pairs={{0,64},{64,128},{128,192},{192,256},{256,320},{320,384},{384,448},... | collective-permute-start | bytes 15368 | tf_op jit(solution)/shard_map/ppermute | solution.py:21
  115.3 33.7 %collective-permute-start.1 = (f32[1,1280]{1,0:T(1,128)}, f32[1,1280]{1,0:T(1,128)}, u32[]{:S(2)}, u32[]{:S(2)}) collective-permute-start(f32[1,1280]{1,0:T(1,128)} %slice.51), channel_id=1, source_target_pairs={{64,0},{128,64},{192,128},{256,192},{320,256},{384,320},{448,384},... | collective-permute-start | bytes 15368 | tf_op jit(solution)/shard_map/ppermute | solution.py:22
  116.6 10.4 %copy-start.55 = (pred[16]{0:T(512)(128)(4,1)}, pred[16]{0:T(512)(128)(4,1)S(1)}, u32[]{:S(2)}) copy-start(pred[16]{0:T(512)(128)(4,1)S(1)} %get-tuple-element.6) | copy-start | bytes 52
  116.6 10.4 %copy-start.57 = (pred[16]{0:T(512)(128)(4,1)}, pred[16]{0:T(512)(128)(4,1)S(1)}, u32[]{:S(2)}) copy-start(pred[16]{0:T(512)(128)(4,1)S(1)} %get-tuple-element.18) | copy-start | bytes 52
  118.1 19.3 %copy-start.67 = (s32[1,80]{1,0:T(1,128)S(1)}, s32[1,80]{1,0:T(1,128)}, u32[]{:S(2)}) copy-start(s32[1,80]{1,0:T(1,128)} %param.45) | copy-start | bytes 964
  118.1 19.3 %copy-start.62 = (s32[1,384]{1,0:T(1,128)S(1)}, s32[1,384]{1,0:T(1,128)}, u32[]{:S(2)}) copy-start(s32[1,384]{1,0:T(1,128)} %param.43) | copy-start | bytes 4612
  118.1 19.4 %copy-start.39 = (s32[6,128]{1,0:T(8,128)S(1)}, s32[6,128]{1,0:T(8,128)}, u32[]{:S(2)}) copy-start(s32[6,128]{1,0:T(8,128)} %param.38) | copy-start | bytes 9220
  118.1 42.5 %collective-permute-start.2 = (f32[1,1280]{1,0:T(1,128)}, f32[1,1280]{1,0:T(1,128)}, u32[]{:S(2)}, u32[]{:S(2)}) collective-permute-start(f32[1,1280]{1,0:T(1,128)} %slice.53), channel_id=1, source_target_pairs={{0,1},{1,2},{2,3},{3,4},{4,5},{5,6},{6,7},{7,8},{8,9},{9,10},{10,1... | collective-permute-start | bytes 15368 | tf_op jit(solution)/shard_map/ppermute | solution.py:21
  121.2 3.3 copy-start.45
  122.7 38.8 %collective-permute-start.3 = (f32[1,1280]{1,0:T(1,128)}, f32[1,1280]{1,0:T(1,128)}, u32[]{:S(2)}, u32[]{:S(2)}) collective-permute-start(f32[1,1280]{1,0:T(1,128)} %slice.55), channel_id=1, source_target_pairs={{1,0},{2,1},{3,2},{4,3},{5,4},{6,5},{7,6},{8,7},{9,8},{10,9},{11,1... | collective-permute-start | bytes 15368 | tf_op jit(solution)/shard_map/ppermute | solution.py:22
  124.6 13.6 %copy-start.47 = (pred[384]{0:T(512)(128)(4,1)}, pred[384]{0:T(512)(128)(4,1)S(1)}, u32[]{:S(2)}) copy-start(pred[384]{0:T(512)(128)(4,1)S(1)} %compare_and_fusion.3) | copy-start | bytes 1156
  124.7 13.6 %copy-start.37 = (s32[1024]{0:T(1024)}, s32[1024]{0:T(1024)S(1)}, u32[]{:S(2)}) copy-start(s32[1024]{0:T(1024)S(1)} %pad_clamp_fusion.3) | copy-start | bytes 12292
  124.7 13.6 %copy-start.32 = (f32[75,128]{1,0:T(8,128)S(1)}, f32[75,128]{1,0:T(8,128)}, u32[]{:S(2)}) copy-start(f32[75,128]{1,0:T(8,128)} %param.34) | copy-start | bytes 115204
  126.0 12.9 %copy-start.63 = (s32[1,384]{1,0:T(1,128)S(1)}, s32[1,384]{1,0:T(1,128)}, u32[]{:S(2)}) copy-start(s32[1,384]{1,0:T(1,128)} %param.44) | copy-start | bytes 4612
  127.0 12.6 %copy-start.64 = (s32[1,384]{1,0:T(1,128)S(1)}, s32[1,384]{1,0:T(1,128)}, u32[]{:S(2)}) copy-start(s32[1,384]{1,0:T(1,128)} %param.42) | copy-start | bytes 4612
  127.0 22.8 %all-to-all-start = ((f32[64,1,480]{2,1,0:T(1,128)}), f32[64,1,480]{2,1,0:T(1,128)}, u32[]{:S(2)}, u32[]{:S(2)}) async-start(f32[64,1,480]{2,1,0:T(1,128)} %reshape.387), calls=%async_computation | async-start | bytes 262144 | tf_op jit(solution)/shard_map/all_to_all | solution.py:257
  137.4 6.8 copy-start.59
  137.4 8.0 %copy-start.49 = (pred[384]{0:T(512)(128)(4,1)}, pred[384]{0:T(512)(128)(4,1)S(1)}, u32[]{:S(2)}) copy-start(pred[384]{0:T(512)(128)(4,1)S(1)} %compare_and_fusion.1) | copy-start | bytes 1156
  138.9 38.0 %copy-start.28 = (f32[4,384]{1,0:T(4,128)}, f32[4,384]{1,0:T(4,128)S(1)}, u32[]{:S(2)}) copy-start(f32[4,384]{1,0:T(4,128)S(1)} %fusion.27) | copy-start | bytes 18436
  138.9 3.3 copy-start.46
  139.6 4.7 copy-start.35
  139.6 33.7 %copy-start.26 = (f32[4,384]{1,0:T(4,128)}, f32[4,384]{1,0:T(4,128)S(1)}, u32[]{:S(2)}) copy-start(f32[4,384]{1,0:T(4,128)S(1)} %fusion.28) | copy-start | bytes 18436
  139.6 2.6 copy-start.17
  149.8 20.9 %all-to-all-start.1 = ((f32[64,1,480]{2,1,0:T(1,128)}), f32[64,1,480]{2,1,0:T(1,128)S(1)}, u32[]{:S(2)}, u32[]{:S(2)}) async-start(f32[64,1,480]{2,1,0:T(1,128)} %reshape.389), calls=%async_computation.1 | async-start | bytes 262144 | tf_op jit(solution)/shard_map/all_to_all | solution.py:258
  166.3 7.0 copy-start.22
  171.8 5.1 copy-start.24
  173.3 6.4 copy-start.30
  173.3 7.8 %copy-start.33 = (s32[1024]{0:T(1024)S(1)}, s32[1024]{0:T(1024)}, u32[]{:S(2)}) copy-start(s32[1024]{0:T(1024)} %pad_clamp_fusion) | copy-start | bytes 12292
  180.1 4.5 copy-start.7
  180.1 4.5 copy-start.40
  183.4 3.0 copy-start.12
  183.4 3.2 copy-start.19
  185.3 2.5 copy-start.1
  185.3 2.5 copy-start.10
  186.4 2.0 copy-start.4
  387.2 2.9 copy-start.38
  394.3 3.7 copy-start.18
  394.3 5.0 copy-start.52
  394.3 5.0 copy-start.54
  394.3 9.5 %copy-start.56 = (pred[16]{0:T(512)(128)(4,1)S(1)}, pred[16]{0:T(512)(128)(4,1)}, u32[]{:S(2)}) copy-start(pred[16]{0:T(512)(128)(4,1)} %copy-done.55) | copy-start | bytes 52
  394.3 9.5 %copy-start.58 = (pred[16]{0:T(512)(128)(4,1)S(1)}, pred[16]{0:T(512)(128)(4,1)}, u32[]{:S(2)}) copy-start(pred[16]{0:T(512)(128)(4,1)} %copy-done.57) | copy-start | bytes 52
  398.0 11.0 %copy-start.16 = (f32[384,80]{1,0:T(8,128)S(1)}, f32[384,80]{1,0:T(8,128)}, u32[]{:S(2)}) copy-start(f32[384,80]{1,0:T(8,128)} %gather_fusion.12) | copy-start | bytes 368644
  398.0 11.0 %copy-start.48 = (pred[384]{0:T(512)(128)(4,1)S(1)}, pred[384]{0:T(512)(128)(4,1)}, u32[]{:S(2)}) copy-start(pred[384]{0:T(512)(128)(4,1)} %copy-done.47) | copy-start | bytes 1156
  398.0 22.1 %copy-start.60 = (pred[80]{0:T(512)(128)(4,1)S(1)}, pred[80]{0:T(512)(128)(4,1)}, u32[]{:S(2)}) copy-start(pred[80]{0:T(512)(128)(4,1)} %copy-done.59) | copy-start | bytes 244
  398.0 22.2 %copy-start.36 = (s32[1024]{0:T(1024)S(1)}, s32[1024]{0:T(1024)}, u32[]{:S(2)}) copy-start(s32[1024]{0:T(1024)} %copy-done.35) | copy-start | bytes 12292
  399.3 22.1 %copy-start.50 = (pred[384]{0:T(512)(128)(4,1)S(1)}, pred[384]{0:T(512)(128)(4,1)}, u32[]{:S(2)}) copy-start(pred[384]{0:T(512)(128)(4,1)} %copy-done.49) | copy-start | bytes 1156
  399.6 23.0 %collective-permute-start.4 = (f32[1,1280]{1,0:T(1,128)S(1)}, f32[1,1280]{1,0:T(1,128)S(1)}, u32[]{:S(2)}, u32[]{:S(2)}) collective-permute-start(f32[1,1280]{1,0:T(1,128)S(1)} %slice.56), channel_id=1, source_target_pairs={{0,64},{64,128},{128,192},{192,256},{256,320},{320,384},{384,448},... | collective-permute-start | bytes 15368 | tf_op jit(solution)/shard_map/ppermute | solution.py:21
  402.5 20.2 %collective-permute-start.5 = (f32[1,1280]{1,0:T(1,128)S(1)}, f32[1,1280]{1,0:T(1,128)S(1)}, u32[]{:S(2)}, u32[]{:S(2)}) collective-permute-start(f32[1,1280]{1,0:T(1,128)S(1)} %slice.57), channel_id=1, source_target_pairs={{64,0},{128,64},{192,128},{256,192},{320,256},{384,320},{448,384},... | collective-permute-start | bytes 15368 | tf_op jit(solution)/shard_map/ppermute | solution.py:22
  404.1 18.8 %collective-permute-start.6 = (f32[1,1280]{1,0:T(1,128)S(1)}, f32[1,1280]{1,0:T(1,128)S(1)}, u32[]{:S(2)}, u32[]{:S(2)}) collective-permute-start(f32[1,1280]{1,0:T(1,128)S(1)} %slice.58), channel_id=1, source_target_pairs={{0,1},{1,2},{2,3},{3,4},{4,5},{5,6},{6,7},{7,8},{8,9},{9,10},{10,1... | collective-permute-start | bytes 15368 | tf_op jit(solution)/shard_map/ppermute | solution.py:21
  406.3 16.9 %collective-permute-start.7 = (f32[1,1280]{1,0:T(1,128)S(1)}, f32[1,1280]{1,0:T(1,128)S(1)}, u32[]{:S(2)}, u32[]{:S(2)}) collective-permute-start(f32[1,1280]{1,0:T(1,128)S(1)} %slice.59), channel_id=1, source_target_pairs={{1,0},{2,1},{3,2},{4,3},{5,4},{6,5},{7,6},{8,7},{9,8},{10,9},{11,1... | collective-permute-start | bytes 15368 | tf_op jit(solution)/shard_map/ppermute | solution.py:22
  410.2 20.3 %all-to-all-start.2 = ((f32[64,1,480]{2,1,0:T(1,128)}), f32[64,1,480]{2,1,0:T(1,128)S(1)}, u32[]{:S(2)}, u32[]{:S(2)}) async-start(f32[64,1,480]{2,1,0:T(1,128)} %reshape.391), calls=%async_computation.2 | async-start | bytes 262144 | tf_op jit(solution)/shard_map/all_to_all | solution.py:257
  422.8 14.8 %copy-start.25 = (f32[4,16,16,1]{2,1,0,3:T(8,128)S(1)}, f32[4,16,16,1]{2,1,0,3:T(8,128)}, u32[]{:S(2)}) copy-start(f32[4,16,16,1]{2,1,0,3:T(8,128)} %constant.90) | copy-start | bytes 12292
  430.5 15.8 %all-to-all-start.3 = ((f32[64,1,480]{2,1,0:T(1,128)}), f32[64,1,480]{2,1,0:T(1,128)}, u32[]{:S(2)}, u32[]{:S(2)}) async-start(f32[64,1,480]{2,1,0:T(1,128)} %reshape.393), calls=%async_computation.3 | async-start | bytes 262144 | tf_op jit(solution)/shard_map/all_to_all | solution.py:258
  437.5 11.1 %copy-start.23 = (f32[4,16,16,1]{2,1,0,3:T(8,128)S(1)}, f32[4,16,16,1]{2,1,0,3:T(8,128)}, u32[]{:S(2)}) copy-start(f32[4,16,16,1]{2,1,0,3:T(8,128)} %constant.91) | copy-start | bytes 12292
  437.5 11.1 %copy-start.27 = (f32[4,384]{1,0:T(4,128)S(1)}, f32[4,384]{1,0:T(4,128)}, u32[]{:S(2)}) copy-start(f32[4,384]{1,0:T(4,128)} %copy-done.26) | copy-start | bytes 18436
  448.3 3.2 copy-start.34
  451.5 1.9 copy-start.13
  (16 other events, 18.0 us)
where the time goes:
time: 760 us; the launch traced here: 749 us
  blocking collectives  584 us (77%)
  starting transfers between devices  53.4 us (7%)
  local copies, waits for them, and re-layouts  38 us (5%)
  matrix products  29.3 us (4%)
  other arithmetic  17.9 us (2%)
  waiting for transfers between devices  17.8 us (2%)
  between operations  8.62 us (1%)
    psum x6, blocking collectives, inner_global(): return lax.psum(partial_value, ('gx', 'yz'))  584 us
    all_to_all x2, starting transfers between devices, on_device(): lax.all_to_all(fine_send, 'yz', split_axis=1, concat_axis=1, tiled=True)  20.3 us
    all_to_all x2, starting transfers between devices, on_device(): lax.all_to_all(outgoing, 'yz', split_axis=1, concat_axis=1, tiled=True)  16.3 us
  transfers between devices with their start and end apart: 12, of which 3 were waited for; matrix products, arithmetic and copies ran while one was open for 4% of the time, Pallas kernels for 0%

commit v1 on v0

v1 whole, which is shorter than its diff:
```python
import functools

import jax
import jax.numpy as jnp
import ml_dtypes
import numpy as np
from jax import lax
from jax.experimental import pallas as pl
from jax.experimental.pallas import tpu as pltpu
from jax.sharding import PartitionSpec as P

MESH = pl.DeviceIdType.MESH
F32 = jnp.float32
BF16 = jnp.bfloat16
I32 = jnp.int32

EPSILON = 1e-6
SCALE = 2.0**-10
CAP = 6
FACE = 80
HALO = 16


def split_np(array):
    high = array.astype(np.float32).astype(ml_dtypes.bfloat16)
    low = (array - high.astype(np.float64)).astype(np.float32).astype(ml_dtypes.bfloat16)
    return high, low


def gll_tables():
    inv_root = 1.0 / np.sqrt(5.0)
    points = np.array([-1.0, -inv_root, inv_root, 1.0])
    weights = np.array([1.0, 5.0, 5.0, 1.0]) / 6.0

    def lagrange(at):
        values = np.ones((len(at), 4))
        for j in range(4):
            for m in range(4):
                if m != j:
                    values[:, j] = values[:, j] * (at - points[m]) / (points[j] - points[m])
        return values

    derivative = np.zeros((4, 4))
    for i in range(4):
        for j in range(4):
            for m in range(4):
                if m != j:
                    term = 1.0 / (points[j] - points[m])
                    for n in range(4):
                        if n != j and n != m:
                            term = term * (points[i] - points[n]) / (points[j] - points[n])
                    derivative[i, j] += term
    halves = [lagrange((points - 1.0) / 2.0), lagrange((points + 1.0) / 2.0)]
    projections = [0.5 * (1.0 / weights)[:, None] * h.T * weights[None, :] for h in halves]
    one5, one4 = np.eye(5), np.eye(4)
    fine = np.concatenate(
        [np.kron(one5, np.kron(projections[q // 2], projections[q % 2])) for q in range(4)], axis=1
    )
    coarse = np.concatenate(
        [np.kron(one5, np.kron(halves[q // 2], halves[q % 2])) for q in range(4)], axis=1
    )
    node = np.concatenate(
        [
            np.kron(derivative, np.kron(one4, one4)),
            np.kron(one4, np.kron(derivative, one4)),
            np.kron(one4, np.kron(one4, derivative)),
        ],
        axis=0,
    )
    select = np.zeros((6, FACE, 320))
    for face in range(6):
        fixed = 3 * (face % 2)
        for a in range(5):
            for p in range(4):
                for q in range(4):
                    n = (
                        fixed * 16 + p * 4 + q,
                        p * 16 + fixed * 4 + q,
                        p * 16 + q * 4 + fixed,
                    )[face // 2]
                    select[face, a * 16 + p * 4 + q, a * 64 + n] = 1.0
    node_high, node_low = split_np(node)
    return (
        np.concatenate([node_high, node_high, node_low], axis=1),
        np.concatenate(split_np(fine), axis=0),
        np.concatenate(split_np(coarse), axis=0),
        select.reshape(480, 320).astype(ml_dtypes.bfloat16),
    )


def split(array):
    high = array.astype(BF16)
    return high, (array - high.astype(F32)).astype(BF16)


def mm(a, b):
    return jnp.dot(a, b, preferred_element_type=F32)


def product(a_high, a_low, b):
    b_high, b_low = split(b)
    n = b.shape[1]
    wide = mm(a_high, jnp.concatenate([b_high, b_low], axis=1))
    return wide[:, :n] + wide[:, n:] + mm(a_low, b_high)


def lanes(shape):
    return lax.broadcasted_iota(I32, shape, 1)


def rows(shape):
    return lax.broadcasted_iota(I32, shape, 0)


def stack_rows(parts, count):
    shape = (count, parts[0].shape[1])
    at = rows(shape)
    out = jnp.zeros(shape, F32)
    for i, part in enumerate(parts):
        out = jnp.where(at == i, part.astype(F32), out)
    return out


def onehot(index, shape):
    return jnp.where(index == rows(shape), 1.0, 0.0).astype(BF16)


def kernel(
    n_gx,
    n_yz,
    hang,
    b_ref,
    mass_ref,
    coef_ref,
    flux_ref,
    first_ref,
    final_ref,
    mid_ref,
    adj_ref,
    plane_ref,
    band_ref,
    small_ref,
    outq_ref,
    incm_ref,
    incq_ref,
    cmts_ref,
    node_ref,
    fine_ref,
    coarse_ref,
    select_ref,
    out_ref,
    x_ref,
    recv_ref,
    hx_ref,
    hrecv_ref,
    gx_ref,
    grecv_ref,
    px_ref,
    precv_ref,
    oh_ref,
    near_own_ref,
    near_in_ref,
    pick_ref,
    lift_ref,
    tr_ref,
    u_ref,
    send_sem,
    recv_sem,
):
    g, k = lax.axis_index("gx"), lax.axis_index("yz")
    wide = 8 * n_yz
    slots = CAP * n_yz
    barrier = pltpu.get_barrier_semaphore()

    def greet(i, _):
        pl.semaphore_signal(
            barrier, inc=1, device_id=(g, lax.rem(k + i, n_yz)), device_id_type=MESH
        )
        return 0

    lax.fori_loop(1, n_yz, greet, 0)
    for i in range(1, n_gx):
        pl.semaphore_signal(
            barrier, inc=1, device_id=(lax.rem(g + i, n_gx), k), device_id_type=MESH
        )

    first_high, first_low = split(first_ref[...])
    final_high, final_low = split(final_ref[...])
    select = select_ref[...]
    pick_ref[0] = mm(select, final_high).astype(BF16)
    pick_ref[1] = mm(select, final_low).astype(BF16)

    mid = mid_ref[...]
    weighted = mid * product(first_high, first_low, b_ref[...])

    lane = lanes((1, wide))
    eighth = jnp.bitwise_and(lane, 7)
    live = eighth < CAP
    small = small_ref[...]
    incm = incm_ref[...]
    parts = [
        jnp.right_shift(small, 5),
        jnp.bitwise_and(small, 31),
        outq_ref[...],
        incm,
        incq_ref[...],
    ]
    target = jnp.where(live, CAP * jnp.right_shift(lane, 3) + eighth, -1)
    spread = mm(stack_rows(parts, 16).astype(BF16), onehot(target, (slots, wide)))
    spread = spread.astype(I32)
    fine_col = jnp.where(live, 32 * spread[0:1] + spread[1:2], -1)
    outq = spread[2:3]
    owned = jnp.where(live & (spread[3:4] < hang), spread[3:4], -1)
    incq = spread[4:5]
    cmts = cmts_ref[...]
    parts = [jnp.right_shift(cmts, 5), jnp.bitwise_and(cmts, 31)]
    found = mm(stack_rows(parts, 16).astype(BF16), onehot(owned, (hang, wide))).astype(I32)
    coarse_col = jnp.where(owned >= 0, 32 * found[0:1] + found[1:2], -1)
    plane, band = plane_ref[0], band_ref[0]
    repeat = jnp.where(
        jnp.bitwise_and(lanes((HALO, 128)), HALO - 1) == rows((HALO, 128)), 1.0, 0.0
    ).astype(BF16)
    halo = mm(
        stack_rows([plane[0:1], plane[1:2], band[0:1], band[1:2]], 16).astype(BF16), repeat
    ).astype(I32)
    group = jnp.right_shift(lanes((1, 128)), 4)
    halo_col = jnp.full((1, 128), -1, I32)
    for i in range(4):
        halo_col = jnp.where(group == i, halo[i : i + 1] + 128 * i, halo_col)
    oh_ref[:, 0:wide] = onehot(fine_col, (768, wide))
    oh_ref[:, wide : 2 * wide] = onehot(coarse_col, (768, wide))
    oh_ref[:, 2 * wide :] = onehot(halo_col, (768, 128))

    node = node_ref[...]
    fine_w, coarse_w = fine_ref[...], coarse_ref[...]

    def project(matrix, high, low, quadrant):
        def spread_out(part):
            return jnp.concatenate(
                [jnp.where(quadrant == q, part, 0.0).astype(BF16) for q in range(4)], axis=0
            )

        both = mm(matrix, spread_out(high))
        return both[:FACE] + both[FACE:] + mm(matrix[:FACE], spread_out(low))

    def send(step, u_traces):
        high, low = split(u_traces)
        tr_ref[0:FACE] = jnp.concatenate(
            [high[FACE * f : FACE * (f + 1)] for f in range(6)], axis=1
        )
        tr_ref[FACE:] = jnp.concatenate([low[FACE * f : FACE * (f + 1)] for f in range(6)], axis=1)
        gathered = mm(tr_ref[...], oh_ref[...])
        halo_out = gathered[:FACE, 2 * wide :] + gathered[FACE:, 2 * wide :]
        halo_out = jnp.concatenate([halo_out, jnp.zeros((48, 128), F32)], axis=0).T
        hx_ref[step] = halo_out[0 : 4 * HALO].reshape(4, HALO, 128)
        fine = project(fine_w, gathered[:FACE, :wide], gathered[FACE:, :wide], outq)
        coarse = project(
            coarse_w,
            gathered[:FACE, wide : 2 * wide],
            gathered[FACE:, wide : 2 * wide],
            incq,
        )
        rest = coarse[48:]
        eight = jnp.bitwise_and(lanes((32, wide)), 7)
        tails = []
        for i in range(4):
            tail = jnp.where(eight == 6, pltpu.roll(rest, 6 - i, 1), 0.0)
            if i < 2:
                tail = jnp.where(eight == 7, pltpu.roll(rest, 3 - i, 1), tail)
            tails.append(tail)
        packed = jnp.where(
            jnp.bitwise_and(lanes((128, wide)), 7) < CAP,
            jnp.concatenate([fine, coarse[:48]], axis=0),
            jnp.concatenate(tails, axis=0),
        )
        x_ref[step] = packed.T.reshape(n_yz, 8, 128)
        if step == 0:
            pl.semaphore_wait(barrier, n_yz + n_gx - 2)
        up_g, down_g = lax.rem(g + 1, n_gx), lax.rem(g + n_gx - 1, n_gx)
        up_k, down_k = lax.rem(k + 1, n_yz), lax.rem(k + n_yz - 1, n_yz)
        for source, target, device in (
            (0, 1, (down_g, k)),
            (1, 0, (up_g, k)),
            (2, 3, (g, down_k)),
            (3, 2, (g, up_k)),
        ):
            pltpu.make_async_remote_copy(
                src_ref=hx_ref.at[step, source],
                dst_ref=hrecv_ref.at[step, target],
                send_sem=send_sem.at[step, 0],
                recv_sem=recv_sem.at[step, 0],
                device_id=device,
                device_id_type=MESH,
            ).start()

        def one(i, _):
            m = lax.rem(k + i, n_yz)
            pltpu.make_async_remote_copy(
                src_ref=x_ref.at[step, m],
                dst_ref=recv_ref.at[step, k],
                send_sem=send_sem.at[step, 1],
                recv_sem=recv_sem.at[step, 1],
                device_id=(g, m),
                device_id_type=MESH,
            ).start()
            return 0

        lax.fori_loop(1, n_yz, one, 0)
        recv_ref[step, pl.ds(k, 1)] = x_ref[step, pl.ds(k, 1)]

    def halo_copy(step):
        return pltpu.make_async_remote_copy(
            src_ref=hx_ref.at[step],
            dst_ref=hrecv_ref.at[step],
            send_sem=send_sem.at[step, 0],
            recv_sem=recv_sem.at[step, 0],
            device_id=(g, k),
            device_id_type=MESH,
        )

    def plane_copy(step):
        return pltpu.make_async_remote_copy(
            src_ref=x_ref.at[step, pl.ds(0, n_yz - 1)],
            dst_ref=recv_ref.at[step, pl.ds(0, n_yz - 1)],
            send_sem=send_sem.at[step, 1],
            recv_sem=recv_sem.at[step, 1],
            device_id=(g, k),
            device_id_type=MESH,
        )

    def receive(step):
        halo_copy(step).wait_recv()
        plane_copy(step).wait_recv()
        tiles = recv_ref[step].reshape(wide, 128).T
        eight = jnp.bitwise_and(lanes((32, wide)), 7)
        rest = jnp.zeros((32, wide), F32)
        for c in range(CAP):
            i, column = c % 4, 6 + c // 4
            moved = pltpu.roll(tiles[32 * i : 32 * i + 32], wide - (column - c), 1)
            rest = jnp.where(eight == c, moved, rest)
        halo_in = hrecv_ref[step].reshape(4 * HALO, 128)
        at = jnp.right_shift(rows((4 * HALO, 128)), 4)
        drop = ((at == 0) & (g == 0)) | ((at == 1) & (g == n_gx - 1))
        halo_in = jnp.where(drop, 0.0, halo_in)
        halo_in = jnp.concatenate([halo_in, jnp.zeros((64, 128), F32)], axis=0).T[:FACE]
        values = jnp.concatenate(
            [tiles[:FACE], jnp.concatenate([tiles[FACE:], rest], axis=0), halo_in], axis=1
        )
        high, low = split(values)
        near = mm(jnp.concatenate([high, low], axis=0), near_in_ref[...])
        return near[:FACE] + near[FACE:]

    def volume(u):
        high, low = split(u)

        def side_by_side(part):
            return jnp.concatenate([part[64 * v : 64 * v + 64] for v in range(5)], axis=1)

        high, low = side_by_side(high), side_by_side(low)
        slopes = mm(node, jnp.concatenate([high, low, high], axis=0))
        out = []
        for a in range(5):
            total = mass_ref[64 * a : 64 * a + 64] * u[64 * a : 64 * a + 64]
            for d in range(3):
                for v in range(5):
                    row = d * 25 + a * 5 + v
                    total = (
                        total
                        + flux_ref[row : row + 1]
                        * slopes[64 * d : 64 * d + 64, 128 * v : 128 * v + 128]
                    )
            out.append(total)
        return product(first_high, first_low, jnp.concatenate(out, axis=0))

    def own_near():
        near = mm(tr_ref[...], near_own_ref[...])
        return near[:FACE] + near[FACE:]

    def finish(base, traces, near_own, near_in):
        near = near_own + near_in
        jumps = jnp.concatenate(
            [
                coef_ref[FACE * f : FACE * (f + 1)]
                * (traces[FACE * f : FACE * (f + 1)] - near[:, 128 * f : 128 * f + 128])
                for f in range(6)
            ],
            axis=0,
        )
        return (mid * SCALE) * (base + product(lift_ref[0], lift_ref[1], jumps))

    def fold(a, b):
        return jnp.sum(a * b, axis=0, keepdims=True)

    traces = product(pick_ref[0], pick_ref[1], weighted)
    send(0, traces)
    u_ref[0] = product(final_high, final_low, weighted)
    nt = (((1,), (1,)), ((), ()))
    lift_ref[0] = lax.dot_general(
        first_high, select, nt, preferred_element_type=F32
    ).astype(BF16)
    lift_ref[1] = lax.dot_general(
        first_low, select, nt, preferred_element_type=F32
    ).astype(BF16)
    table = 768 + 4 * HALO
    owned_col = jnp.broadcast_to(jnp.where(owned >= 0, owned + table, -1), (128, wide)).T
    place = rows((wide, 128))
    reply = jnp.where(
        jnp.bitwise_and(place, 7) < CAP,
        CAP * jnp.right_shift(place, 3) + jnp.bitwise_and(place, 7) + table + hang,
        -1,
    )
    halo_at = rows((128, 128))
    halo_at = jnp.where(halo_at < 4 * HALO, halo_at + 768, -1)
    for f in range(6):
        adj = adj_ref[f : f + 1]
        near_own_ref[:, 128 * f : 128 * f + 128] = onehot(adj, (768, 128))
        near_in_ref[0:wide, 128 * f : 128 * f + 128] = jnp.where(
            owned_col == adj, 1.0, 0.0
        ).astype(BF16)
        near_in_ref[wide : 2 * wide, 128 * f : 128 * f + 128] = jnp.where(
            reply == adj, 1.0, 0.0
        ).astype(BF16)
        near_in_ref[2 * wide :, 128 * f : 128 * f + 128] = jnp.where(
            halo_at == adj, 1.0, 0.0
        ).astype(BF16)
    base = volume(u_ref[0])
    near_own = own_near()
    weighted = finish(base, traces, near_own, receive(0))

    traces = product(pick_ref[0], pick_ref[1], weighted)
    send(1, traces)
    u_ref[1] = product(final_high, final_low, weighted)
    base = volume(u_ref[1])
    near_own = own_near()
    r, u1 = u_ref[0], u_ref[1]
    g00, g01, g11 = fold(r, r), fold(r, u1), fold(u1, u1)
    weighted = finish(base, traces, near_own, receive(1))
    u2 = product(final_high, final_low, weighted)

    mine = stack_rows([g00, g01, g11, fold(r, u2), fold(u1, u2), fold(u2, u2)], 8)
    gx_ref[...] = mine
    for i in range(1, n_gx):
        pltpu.make_async_remote_copy(
            src_ref=gx_ref,
            dst_ref=grecv_ref.at[g],
            send_sem=send_sem.at[2, 0],
            recv_sem=recv_sem.at[2, 0],
            device_id=(lax.rem(g + i, n_gx), k),
            device_id_type=MESH,
        ).start()
    grecv_ref[pl.ds(g, 1)] = mine.reshape(1, 8, 128)
    gram_copy = pltpu.make_async_remote_copy(
        src_ref=grecv_ref.at[pl.ds(0, n_gx - 1)],
        dst_ref=grecv_ref.at[pl.ds(0, n_gx - 1)],
        send_sem=send_sem.at[2, 0],
        recv_sem=recv_sem.at[2, 0],
        device_id=(g, k),
        device_id_type=MESH,
    )
    gram_copy.wait_recv()
    column = jnp.sum(jnp.sum(grecv_ref[...], axis=0), axis=1, keepdims=True)
    diagonal = jnp.where(rows((8, 128)) == lanes((8, 128)), column, 0.0)
    mine = jnp.sum(diagonal, axis=0, keepdims=True)
    px_ref[...] = mine

    def one(i, _):
        pltpu.make_async_remote_copy(
            src_ref=px_ref,
            dst_ref=precv_ref.at[k],
            send_sem=send_sem.at[2, 1],
            recv_sem=recv_sem.at[2, 1],
            device_id=(g, lax.rem(k + i, n_yz)),
            device_id_type=MESH,
        ).start()
        return 0

    lax.fori_loop(1, n_yz, one, 0)
    precv_ref[pl.ds(k, 1)] = mine.reshape(1, 1, 128)
    sum_copy = pltpu.make_async_remote_copy(
        src_ref=precv_ref.at[pl.ds(0, n_yz - 1)],
        dst_ref=precv_ref.at[pl.ds(0, n_yz - 1)],
        send_sem=send_sem.at[2, 1],
        recv_sem=recv_sem.at[2, 1],
        device_id=(g, k),
        device_id_type=MESH,
    )
    sum_copy.wait_recv()
    total = jnp.sum(precv_ref[...], axis=0)
    at = lanes((1, 128))

    def entry(i):
        return jnp.sum(jnp.where(at == i, total, 0.0), axis=1, keepdims=True)

    c_r, c_u = coefficients(*[entry(i) for i in range(6)])
    out_ref[...] = c_r * u_ref[0] + c_u * u_ref[1]

    for step in range(2):
        halo_copy(step).wait_send()
        plane_copy(step).wait_send()
    gram_copy.wait_send()
    sum_copy.wait_send()


def coefficients(g00, g01, g11, g02, g12, g22):
    s = SCALE
    beta = jnp.sqrt(g00 + EPSILON)
    h00 = g01 / (s * beta * beta)
    p1, p0 = 1.0 / s, -h00
    norm = (p1 * p1 * g11 + 2.0 * p1 * p0 * g01 + p0 * p0 * g00) / (beta * beta)
    h10 = jnp.sqrt(jnp.maximum(norm, 0.0) + EPSILON)
    c1, c0 = p1 / (beta * h10), p0 / (beta * h10)
    a2, a1 = c1 / s, c0 / s
    h01 = (a2 * g02 + a1 * g01) / beta
    a0 = -h01 / beta
    h11 = c1 * (a2 * g12 + a1 * g11 + a0 * g01) + c0 * (a2 * g02 + a1 * g01 + a0 * g00)
    a1, a0 = a1 - h11 * c1, a0 - h11 * c0
    norm = a2 * (a2 * g22 + 2.0 * (a1 * g12 + a0 * g02)) + (
        a1 * (a1 * g11 + 2.0 * a0 * g01) + a0 * a0 * g00
    )
    h21 = jnp.sqrt(jnp.maximum(norm, 0.0) + EPSILON)
    radius = jnp.sqrt(h00 * h00 + h10 * h10)
    cos0, sin0 = h00 / radius, h10 / radius
    top = cos0 * h01 + sin0 * h11
    low = cos0 * h11 - sin0 * h01
    length = jnp.sqrt(low * low + h21 * h21)
    y1 = (low / length) * (-sin0 * beta) / length
    y0 = (cos0 * beta - top * y1) / radius
    return y0 / beta + y1 * c0, y1 * c1


def on_device(
    n_gx,
    n_yz,
    source,
    mass,
    coupling,
    flux,
    first,
    final,
    middle,
    adjacent,
    plane,
    band,
    small,
    proprietor,
    outq,
    incm,
    incq,
    cmts,
):
    del proprietor
    tables = [jnp.asarray(t) for t in gll_tables()]
    wide = 8 * n_yz
    arguments = (
        source, mass, coupling, flux, first, final, middle, adjacent, plane, band,
        small, outq, incm, incq, cmts, *tables,
    )
    vmem = pl.BlockSpec(memory_space=pltpu.VMEM)
    return pl.pallas_call(
        functools.partial(kernel, n_gx, n_yz, cmts.shape[1]),
        out_shape=jax.ShapeDtypeStruct(source.shape, F32),
        in_specs=[vmem] * len(arguments),
        out_specs=vmem,
        scratch_shapes=[
            pltpu.VMEM((2, n_yz, 8, 128), F32),
            pltpu.VMEM((2, n_yz, 8, 128), F32),
            pltpu.VMEM((2, 4, HALO, 128), F32),
            pltpu.VMEM((2, 4, HALO, 128), F32),
            pltpu.VMEM((8, 128), F32),
            pltpu.VMEM((n_gx, 8, 128), F32),
            pltpu.VMEM((1, 128), F32),
            pltpu.VMEM((n_yz, 1, 128), F32),
            pltpu.VMEM((768, 2 * wide + 128), BF16),
            pltpu.VMEM((768, 768), BF16),
            pltpu.VMEM((2 * wide + 128, 768), BF16),
            pltpu.VMEM((2, 480, 320), BF16),
            pltpu.VMEM((2, 320, 480), BF16),
            pltpu.VMEM((2 * FACE, 768), BF16),
            pltpu.VMEM((2, 320, 128), F32),
            pltpu.SemaphoreType.DMA((3, 2)),
            pltpu.SemaphoreType.DMA((3, 2)),
        ],
        compiler_params=pltpu.CompilerParams(
            collective_id=0, has_side_effects=True, vmem_limit_bytes=48 * 1024 * 1024
        ),
    )(*arguments)


def solution(mesh):
    n_gx, n_yz = mesh.shape["gx"], mesh.shape["yz"]
    both = ("gx", "yz")
    field, lists = P(None, both), P(both, None)
    return jax.shard_map(
        functools.partial(on_device, n_gx, n_yz),
        mesh=mesh,
        in_specs=(
            field, field, field, field, P(), P(), field, field,
            P(both, None, None), P(both, None, None),
            lists, lists, lists, lists, lists, lists,
        ),
        out_specs=field,
        check_vma=False,
    )
```

time: 760 us -> 66.7 us (0.09); the launches traced: 749 us -> 66.1 us
  blocking collectives: 584 us -> 0 us
  starting transfers between devices: 53.4 us -> 0 us
  Pallas kernels: 0 us -> 49.7 us
  matrix products: 29.3 us -> 0 us
  local copies, waits for them, and re-layouts: 38 us -> 16.3 us
  other arithmetic: 17.9 us -> 0 us
  waiting for transfers between devices: 17.8 us -> 0 us
  between operations: 8.62 us -> 0.03 us
    psum x6 -> x0, blocking collectives: 584 us -> none  [inner_global(): return lax.psum(partial_value, ('gx', 'yz'))]
    pallas_call x0 -> x1, Pallas kernels: none -> 49.7 us  [on_device(): pl.pallas_call(functools.partial(kernel, n_gx, n_yz, cmts.shape[1]), out_...]
    all_to_all x4 -> x0, starting transfers between devices: 36.5 us -> none  [the longest x2 20.3 us: on_device(): lax.all_to_all(fine_send, 'yz', split_axis=1, concat_axis=1, tiled=True)]
    dot_general x20 -> x0, matrix products: 29.3 us -> none  [the longest x2 6.24 us: jacobian(): jnp.einsum('dabe,bne->dane', flux_blocks, nodal_view, precision=maximum_d...]
    all_to_all x4 -> x0, waiting for transfers between devices: 17.8 us -> none  [the longest x2 10.6 us: on_device(): lax.all_to_all(outgoing, 'yz', split_axis=1, concat_axis=1, tiled=True)]
    ppermute x8 -> x0, starting transfers between devices: 16.9 us -> none  [the longest x4 9.64 us: with_halo(): before = lax.ppermute(last, axis, up)]
    gather x18 -> x0, local copies, waits for them, and re-layouts: 16.5 us -> none  [the longest x4 5.18 us: on_device(): jnp.take(trace_table, near_index, axis=1, mode='fill', fill_value=0.0)]
    unnamed x156 -> x39, local copies, waits for them, and re-layouts: 6.74 us -> 16.3 us
  transfers between devices with their start and end apart: 12 -> 0, of which waited for: 3 -> 0; matrix products, arithmetic and copies ran while one was open for 4% -> 0% of each run, Pallas kernels for 0% -> 0%
where the time goes in v1:
time: 66.7 us; the launch traced here: 66.1 us
  Pallas kernels  49.7 us (75%)
  local copies, waits for them, and re-layouts  16.3 us (24%)
    pallas_call x1, Pallas kernels, on_device(): pl.pallas_call(functools.partial(kernel, n_gx, n_yz, cmts.shape[1]), out_...  49.7 us
    unnamed x39, local copies, waits for them, and re-layouts  16.3 us

profile of v1, /device:TPU:1, one launch (start us, length us, event | category | flops | bytes accessed | tf_op | source)
XLA Modules:
  0.0 66.1 jit_solution(12490106232658894575)
XLA Ops:
  0.0 0.0 copy-start
  0.0 1.0 %copy-done = f32[320,320]{1,0:T(8,128)S(1)} copy-done((f32[320,320]{1,0:T(8,128)S(1)}, f32[320,320]{1,0:T(8,128)}, u32[]{:S(2)}) %copy-start) | copy-done | bytes 409624
  1.0 0.0 copy-start.1
  1.0 1.0 %copy-done.1 = f32[320,320]{1,0:T(8,128)S(1)} copy-done((f32[320,320]{1,0:T(8,128)S(1)}, f32[320,320]{1,0:T(8,128)}, u32[]{:S(2)}) %copy-start.1) | copy-done | bytes 409624
  2.1 0.0 copy-start.2
  2.1 1.0 %copy-done.2 = bf16[480,320]{1,0:T(8,128)(2,1)S(1)} copy-done((bf16[480,320]{1,0:T(8,128)(2,1)S(1)}, bf16[480,320]{1,0:T(8,128)(2,1)}, u32[]{:S(2)}) %copy-start.2) | copy-done | bytes 307224
  3.0 0.0 copy-start.3
  3.1 0.9 %copy-done.3 = f32[480,128]{1,0:T(8,128)S(1)} copy-done((f32[480,128]{1,0:T(8,128)S(1)}, f32[480,128]{1,0:T(8,128)}, u32[]{:S(2)}) %copy-start.3) | copy-done | bytes 245784
  4.0 0.0 copy-start.4
  4.0 0.9 %copy-done.4 = f32[320,128]{1,0:T(8,128)S(1)} copy-done((f32[320,128]{1,0:T(8,128)S(1)}, f32[320,128]{1,0:T(8,128)}, u32[]{:S(2)}) %copy-start.4) | copy-done | bytes 163864
  4.9 0.0 copy-start.5
  4.9 0.9 %copy-done.5 = f32[320,128]{1,0:T(8,128)S(1)} copy-done((f32[320,128]{1,0:T(8,128)S(1)}, f32[320,128]{1,0:T(8,128)}, u32[]{:S(2)}) %copy-start.5) | copy-done | bytes 163864
  5.8 0.0 copy-start.6
  5.8 0.9 %copy-done.6 = f32[320,128]{1,0:T(8,128)S(1)} copy-done((f32[320,128]{1,0:T(8,128)S(1)}, f32[320,128]{1,0:T(8,128)}, u32[]{:S(2)}) %copy-start.6) | copy-done | bytes 163864
  6.7 0.0 copy-start.7
  6.7 0.9 %copy-done.7 = bf16[160,320]{1,0:T(8,128)(2,1)S(1)} copy-done((bf16[160,320]{1,0:T(8,128)(2,1)S(1)}, bf16[160,320]{1,0:T(8,128)(2,1)}, u32[]{:S(2)}) %copy-start.7) | copy-done | bytes 102424
  7.6 0.0 copy-start.8
  7.6 0.9 %copy-done.8 = bf16[160,320]{1,0:T(8,128)(2,1)S(1)} copy-done((bf16[160,320]{1,0:T(8,128)(2,1)S(1)}, bf16[160,320]{1,0:T(8,128)(2,1)}, u32[]{:S(2)}) %copy-start.8) | copy-done | bytes 102424
  8.5 0.0 copy-start.9
  8.5 0.9 %copy-done.9 = bf16[192,192]{1,0:T(8,128)(2,1)S(1)} copy-done((bf16[192,192]{1,0:T(8,128)(2,1)S(1)}, bf16[192,192]{1,0:T(8,128)(2,1)}, u32[]{:S(2)}) %copy-start.9) | copy-done | bytes 73752
  9.4 0.0 copy-start.10
  9.4 0.8 %copy-done.10 = f32[75,128]{1,0:T(8,128)S(1)} copy-done((f32[75,128]{1,0:T(8,128)S(1)}, f32[75,128]{1,0:T(8,128)}, u32[]{:S(2)}) %copy-start.10) | copy-done | bytes 38424
  10.2 0.0 copy-start.11
  10.2 0.7 %copy-done.11 = s32[6,128]{1,0:T(8,128)S(1)} copy-done((s32[6,128]{1,0:T(8,128)S(1)}, s32[6,128]{1,0:T(8,128)}, u32[]{:S(2)}) %copy-start.11) | copy-done | bytes 3096
  10.9 0.0 copy-start.12
  10.9 0.7 %copy-done.12 = s32[1,384]{1,0:T(1,128)S(1)} copy-done((s32[1,384]{1,0:T(1,128)S(1)}, s32[1,384]{1,0:T(1,128)}, u32[]{:S(2)}) %copy-start.12) | copy-done | bytes 1560
  11.6 0.0 copy-start.13
  11.6 0.7 %copy-done.13 = s32[1,384]{1,0:T(1,128)S(1)} copy-done((s32[1,384]{1,0:T(1,128)S(1)}, s32[1,384]{1,0:T(1,128)}, u32[]{:S(2)}) %copy-start.13) | copy-done | bytes 1560
  12.3 0.0 copy-start.14
  12.3 0.7 %copy-done.14 = s32[1,384]{1,0:T(1,128)S(1)} copy-done((s32[1,384]{1,0:T(1,128)S(1)}, s32[1,384]{1,0:T(1,128)}, u32[]{:S(2)}) %copy-start.14) | copy-done | bytes 1560
  12.9 0.0 copy-start.15
  13.0 0.7 %copy-done.15 = s32[1,384]{1,0:T(1,128)S(1)} copy-done((s32[1,384]{1,0:T(1,128)S(1)}, s32[1,384]{1,0:T(1,128)}, u32[]{:S(2)}) %copy-start.15) | copy-done | bytes 1560
  13.6 0.0 copy-start.16
  13.6 0.7 %copy-done.16 = s32[1,2,16]{2,1,0:T(2,128)S(1)} copy-done((s32[1,2,16]{2,1,0:T(2,128)S(1)}, s32[1,2,16]{2,1,0:T(2,128)}, u32[]{:S(2)}) %copy-start.16) | copy-done | bytes 152
  14.3 0.0 copy-start.17
  14.3 0.7 %copy-done.17 = s32[1,2,16]{2,1,0:T(2,128)S(1)} copy-done((s32[1,2,16]{2,1,0:T(2,128)S(1)}, s32[1,2,16]{2,1,0:T(2,128)}, u32[]{:S(2)}) %copy-start.17) | copy-done | bytes 152
  15.0 0.0 copy-start.18
  15.0 0.7 copy-done.18
  15.6 49.7 %shard_map.181 = f32[320,128]{1,0:T(8,128)S(1)} custom-call(f32[320,128]{1,0:T(8,128)S(1)} %copy-done.4, f32[320,128]{1,0:T(8,128)S(1)} %copy-done.5, f32[480,128]{1,0:T(8,128)S(1)} %copy-done.3, f32[75,128]{1,0:T(8,128)S(1)} %copy-done.10, f32[320,320]{1,0:T(8,128)S(1)} %copy-done, f32[320,320]{1,0:T(8,128)S(1)} %copy-done.1, f32[320,128]{1,0:T(8,128)S(1)} %copy-done.6, ...), custom_call_target="tpu_custom_call" | custom-call | tf_op jit(solution)/shard_map/pallas_call | solution.py:559
  65.4 0.7 %copy.21 = f32[320,128]{1,0:T(8,128)} copy(f32[320,128]{1,0:T(8,128)S(1)} %shard_map.181) | data formatting | bytes 327680
Async XLA Ops:
  0.0 1.0 %copy-start = (f32[320,320]{1,0:T(8,128)S(1)}, f32[320,320]{1,0:T(8,128)}, u32[]{:S(2)}) copy-start(f32[320,320]{1,0:T(8,128)} %first_ref.1) | copy-start | bytes 1228804
  1.0 1.0 %copy-start.1 = (f32[320,320]{1,0:T(8,128)S(1)}, f32[320,320]{1,0:T(8,128)}, u32[]{:S(2)}) copy-start(f32[320,320]{1,0:T(8,128)} %final_ref.1) | copy-start | bytes 1228804
  2.1 1.0 %copy-start.2 = (bf16[480,320]{1,0:T(8,128)(2,1)S(1)}, bf16[480,320]{1,0:T(8,128)(2,1)}, u32[]{:S(2)}) copy-start(bf16[480,320]{1,0:T(8,128)(2,1)} %constant.11.clone.select_ref) | copy-start | bytes 921604
  3.0 0.9 %copy-start.3 = (f32[480,128]{1,0:T(8,128)S(1)}, f32[480,128]{1,0:T(8,128)}, u32[]{:S(2)}) copy-start(f32[480,128]{1,0:T(8,128)} %coef_ref.1) | copy-start | bytes 737284
  4.0 0.9 %copy-start.4 = (f32[320,128]{1,0:T(8,128)S(1)}, f32[320,128]{1,0:T(8,128)}, u32[]{:S(2)}) copy-start(f32[320,128]{1,0:T(8,128)} %b_ref.1) | copy-start | bytes 491524
  4.9 0.9 %copy-start.5 = (f32[320,128]{1,0:T(8,128)S(1)}, f32[320,128]{1,0:T(8,128)}, u32[]{:S(2)}) copy-start(f32[320,128]{1,0:T(8,128)} %mass_ref.1) | copy-start | bytes 491524
  5.8 0.9 %copy-start.6 = (f32[320,128]{1,0:T(8,128)S(1)}, f32[320,128]{1,0:T(8,128)}, u32[]{:S(2)}) copy-start(f32[320,128]{1,0:T(8,128)} %mid_ref.1) | copy-start | bytes 491524
  6.7 0.9 %copy-start.7 = (bf16[160,320]{1,0:T(8,128)(2,1)S(1)}, bf16[160,320]{1,0:T(8,128)(2,1)}, u32[]{:S(2)}) copy-start(bf16[160,320]{1,0:T(8,128)(2,1)} %constant.10.clone.coarse_ref) | copy-start | bytes 307204
  7.6 0.9 %copy-start.8 = (bf16[160,320]{1,0:T(8,128)(2,1)S(1)}, bf16[160,320]{1,0:T(8,128)(2,1)}, u32[]{:S(2)}) copy-start(bf16[160,320]{1,0:T(8,128)(2,1)} %constant.9.clone.fine_ref) | copy-start | bytes 307204
  8.5 0.9 %copy-start.9 = (bf16[192,192]{1,0:T(8,128)(2,1)S(1)}, bf16[192,192]{1,0:T(8,128)(2,1)}, u32[]{:S(2)}) copy-start(bf16[192,192]{1,0:T(8,128)(2,1)} %constant.8.clone.node_ref) | copy-start | bytes 221188
  9.4 0.8 %copy-start.10 = (f32[75,128]{1,0:T(8,128)S(1)}, f32[75,128]{1,0:T(8,128)}, u32[]{:S(2)}) copy-start(f32[75,128]{1,0:T(8,128)} %flux_ref.1) | copy-start | bytes 115204
  10.2 0.7 %copy-start.11 = (s32[6,128]{1,0:T(8,128)S(1)}, s32[6,128]{1,0:T(8,128)}, u32[]{:S(2)}) copy-start(s32[6,128]{1,0:T(8,128)} %adj_ref.1) | copy-start | bytes 9220
  10.9 0.7 %copy-start.12 = (s32[1,384]{1,0:T(1,128)S(1)}, s32[1,384]{1,0:T(1,128)}, u32[]{:S(2)}) copy-start(s32[1,384]{1,0:T(1,128)} %small_ref.1) | copy-start | bytes 4612
  11.6 0.7 %copy-start.13 = (s32[1,384]{1,0:T(1,128)S(1)}, s32[1,384]{1,0:T(1,128)}, u32[]{:S(2)}) copy-start(s32[1,384]{1,0:T(1,128)} %outq_ref.1) | copy-start | bytes 4612
  12.3 0.7 %copy-start.14 = (s32[1,384]{1,0:T(1,128)S(1)}, s32[1,384]{1,0:T(1,128)}, u32[]{:S(2)}) copy-start(s32[1,384]{1,0:T(1,128)} %incm_ref.1) | copy-start | bytes 4612
  12.9 0.7 %copy-start.15 = (s32[1,384]{1,0:T(1,128)S(1)}, s32[1,384]{1,0:T(1,128)}, u32[]{:S(2)}) copy-start(s32[1,384]{1,0:T(1,128)} %incq_ref.1) | copy-start | bytes 4612
  13.6 0.7 %copy-start.16 = (s32[1,2,16]{2,1,0:T(2,128)S(1)}, s32[1,2,16]{2,1,0:T(2,128)}, u32[]{:S(2)}) copy-start(s32[1,2,16]{2,1,0:T(2,128)} %plane_ref.1) | copy-start | bytes 388
  14.3 0.7 %copy-start.17 = (s32[1,2,16]{2,1,0:T(2,128)S(1)}, s32[1,2,16]{2,1,0:T(2,128)}, u32[]{:S(2)}) copy-start(s32[1,2,16]{2,1,0:T(2,128)} %band_ref.1) | copy-start | bytes 388
  15.0 0.7 copy-start.18

commit v2 on v1

--- a/solution.py
+++ b/solution.py
@@ -125,10 +125,38 @@
     return jnp.where(index == rows(shape), 1.0, 0.0).astype(BF16)
 
 
+def far_first(size):
+    return sorted(range(size), key=lambda d: -min(d, size - d))
+
+
+def outward(i, size):
+    return lax.rem(size // 2 + (i + 1) // 2 * (1 - 2 * lax.rem(i, 2)) + size, size)
+
+
 def kernel(
     n_gx,
     n_yz,
     hang,
+    b_hbm,
+    mass_hbm,
+    coef_hbm,
+    flux_hbm,
+    first_hbm,
+    final_hbm,
+    mid_hbm,
+    adj_hbm,
+    plane_hbm,
+    band_hbm,
+    small_hbm,
+    outq_hbm,
+    incm_hbm,
+    incq_hbm,
+    cmts_hbm,
+    node_hbm,
+    fine_hbm,
+    coarse_hbm,
+    select_hbm,
+    out_ref,
     b_ref,
     mass_ref,
     coef_ref,
@@ -148,7 +176,7 @@
     fine_ref,
     coarse_ref,
     select_ref,
-    out_ref,
+    load_sem,
     x_ref,
     recv_ref,
     hx_ref,
@@ -172,18 +200,69 @@
     slots = CAP * n_yz
     barrier = pltpu.get_barrier_semaphore()
 
-    def greet(i, _):
-        pl.semaphore_signal(
-            barrier, inc=1, device_id=(g, lax.rem(k + i, n_yz)), device_id_type=MESH
-        )
-        return 0
-
-    lax.fori_loop(1, n_yz, greet, 0)
-    for i in range(1, n_gx):
-        pl.semaphore_signal(
-            barrier, inc=1, device_id=(lax.rem(g + i, n_gx), k), device_id_type=MESH
-        )
-
+    n_y = 8 if n_yz % 16 == 0 else n_yz // 2
+    n_x = n_yz // (2 * n_y)
+    x, y, core = k // (2 * n_y), lax.rem(k // 2, n_y), lax.rem(k, 2)
+
+    columns = [
+        (lax.rem(x + dx, n_x) * n_y * 2, dx, c)
+        for dx in far_first(n_x)
+        for c in (1, 0)
+    ]
+    cores = (core, 1 - core)
+
+    def plane(act):
+        def one(i, _):
+            at = lax.rem(y + outward(i, n_y), n_y) * 2
+            for column, _, c in columns:
+                act(column + at + cores[c])
+            return 0
+
+        lax.fori_loop(0, n_y - 1, one, 0)
+        for column, dx, c in columns:
+            if dx or c:
+                act(column + y * 2 + cores[c])
+
+    def greet(device):
+        pl.semaphore_signal(barrier, inc=1, device_id=(g, device), device_id_type=MESH)
+
+    plane(greet)
+    gx_partners = [lax.rem(g + dg, n_gx) for dg in far_first(n_gx) if dg]
+    for partner_g in gx_partners:
+        pl.semaphore_signal(barrier, inc=1, device_id=(partner_g, k), device_id_type=MESH)
+    loads = {}
+    for i, (name, source, target) in enumerate(
+        (
+            ("first", first_hbm, first_ref),
+            ("b", b_hbm, b_ref),
+            ("small", small_hbm, small_ref),
+            ("outq", outq_hbm, outq_ref),
+            ("incm", incm_hbm, incm_ref),
+            ("incq", incq_hbm, incq_ref),
+            ("cmts", cmts_hbm, cmts_ref),
+            ("plane", plane_hbm, plane_ref),
+            ("band", band_hbm, band_ref),
+            ("mid", mid_hbm, mid_ref),
+            ("final", final_hbm, final_ref),
+            ("select", select_hbm, select_ref),
+            ("fine", fine_hbm, fine_ref),
+            ("coarse", coarse_hbm, coarse_ref),
+            ("node", node_hbm, node_ref),
+            ("mass", mass_hbm, mass_ref),
+            ("flux", flux_hbm, flux_ref),
+            ("coef", coef_hbm, coef_ref),
+            ("adj", adj_hbm, adj_ref),
+        )
+    ):
+        loads[name] = pltpu.make_async_copy(source, target, load_sem.at[i])
+        loads[name].start()
+
+    def ready(*wanted):
+        for name in wanted:
+            loads[name].wait()
+
+    ready("first", "b", "small", "outq", "incm", "incq", "cmts", "plane", "band")
+    ready("mid", "final", "select", "fine", "coarse")
     first_high, first_low = split(first_ref[...])
     final_high, final_low = split(final_ref[...])
     select = select_ref[...]
@@ -216,12 +295,12 @@
     parts = [jnp.right_shift(cmts, 5), jnp.bitwise_and(cmts, 31)]
     found = mm(stack_rows(parts, 16).astype(BF16), onehot(owned, (hang, wide))).astype(I32)
     coarse_col = jnp.where(owned >= 0, 32 * found[0:1] + found[1:2], -1)
-    plane, band = plane_ref[0], band_ref[0]
+    slab, side = plane_ref[0], band_ref[0]
     repeat = jnp.where(
         jnp.bitwise_and(lanes((HALO, 128)), HALO - 1) == rows((HALO, 128)), 1.0, 0.0
     ).astype(BF16)
     halo = mm(
-        stack_rows([plane[0:1], plane[1:2], band[0:1], band[1:2]], 16).astype(BF16), repeat
+        stack_rows([slab[0:1], slab[1:2], side[0:1], side[1:2]], 16).astype(BF16), repeat
     ).astype(I32)
     group = jnp.right_shift(lanes((1, 128)), 4)
     halo_col = jnp.full((1, 128), -1, I32)
@@ -231,14 +310,17 @@
     oh_ref[:, wide : 2 * wide] = onehot(coarse_col, (768, wide))
     oh_ref[:, 2 * wide :] = onehot(halo_col, (768, 128))
 
-    node = node_ref[...]
     fine_w, coarse_w = fine_ref[...], coarse_ref[...]
 
-    def project(matrix, high, low, quadrant):
+    def masks(quadrant):
+        return [jnp.where(quadrant == q, 1.0, 0.0).astype(BF16) for q in range(4)]
+
+    out_masks, in_masks = masks(outq), masks(incq)
+
+    def project(matrix, high, low, mask):
         def spread_out(part):
-            return jnp.concatenate(
-                [jnp.where(quadrant == q, part, 0.0).astype(BF16) for q in range(4)], axis=0
-            )
+            part = part.astype(BF16)
+            return jnp.concatenate([part * mask[q] for q in range(4)], axis=0)
 
         both = mm(matrix, spread_out(high))
         return both[:FACE] + both[FACE:] + mm(matrix[:FACE], spread_out(low))
@@ -253,12 +335,12 @@
         halo_out = gathered[:FACE, 2 * wide :] + gathered[FACE:, 2 * wide :]
         halo_out = jnp.concatenate([halo_out, jnp.zeros((48, 128), F32)], axis=0).T
         hx_ref[step] = halo_out[0 : 4 * HALO].reshape(4, HALO, 128)
-        fine = project(fine_w, gathered[:FACE, :wide], gathered[FACE:, :wide], outq)
+        fine = project(fine_w, gathered[:FACE, :wide], gathered[FACE:, :wide], out_masks)
         coarse = project(
             coarse_w,
             gathered[:FACE, wide : 2 * wide],
             gathered[FACE:, wide : 2 * wide],
-            incq,
+            in_masks,
         )
         rest = coarse[48:]
         eight = jnp.bitwise_and(lanes((32, wide)), 7)
@@ -276,6 +358,17 @@
         x_ref[step] = packed.T.reshape(n_yz, 8, 128)
         if step == 0:
             pl.semaphore_wait(barrier, n_yz + n_gx - 2)
+        def one(m):
+            pltpu.make_async_remote_copy(
+                src_ref=x_ref.at[step, m],
+                dst_ref=recv_ref.at[step, k],
+                send_sem=send_sem.at[step, 1],
+                recv_sem=recv_sem.at[step, 1],
+                device_id=(g, m),
+                device_id_type=MESH,
+            ).start()
+
+        plane(one)
         up_g, down_g = lax.rem(g + 1, n_gx), lax.rem(g + n_gx - 1, n_gx)
         up_k, down_k = lax.rem(k + 1, n_yz), lax.rem(k + n_yz - 1, n_yz)
         for source, target, device in (
@@ -292,20 +385,6 @@
                 device_id=device,
                 device_id_type=MESH,
             ).start()
-
-        def one(i, _):
-            m = lax.rem(k + i, n_yz)
-            pltpu.make_async_remote_copy(
-                src_ref=x_ref.at[step, m],
-                dst_ref=recv_ref.at[step, k],
-                send_sem=send_sem.at[step, 1],
-                recv_sem=recv_sem.at[step, 1],
-                device_id=(g, m),
-                device_id_type=MESH,
-            ).start()
-            return 0
-
-        lax.fori_loop(1, n_yz, one, 0)
         recv_ref[step, pl.ds(k, 1)] = x_ref[step, pl.ds(k, 1)]
 
     def halo_copy(step):
@@ -352,6 +431,7 @@
 
     def volume(u):
         high, low = split(u)
+        node = node_ref[...]
 
         def side_by_side(part):
             return jnp.concatenate([part[64 * v : 64 * v + 64] for v in range(5)], axis=1)
@@ -401,6 +481,7 @@
     lift_ref[1] = lax.dot_general(
         first_low, select, nt, preferred_element_type=F32
     ).astype(BF16)
+    ready("node", "mass", "flux", "coef", "adj")
     table = 768 + 4 * HALO
     owned_col = jnp.broadcast_to(jnp.where(owned >= 0, owned + table, -1), (128, wide)).T
     place = rows((wide, 128))
@@ -439,13 +520,13 @@
 
     mine = stack_rows([g00, g01, g11, fold(r, u2), fold(u1, u2), fold(u2, u2)], 8)
     gx_ref[...] = mine
-    for i in range(1, n_gx):
+    for partner_g in gx_partners:
         pltpu.make_async_remote_copy(
             src_ref=gx_ref,
             dst_ref=grecv_ref.at[g],
             send_sem=send_sem.at[2, 0],
             recv_sem=recv_sem.at[2, 0],
-            device_id=(lax.rem(g + i, n_gx), k),
+            device_id=(partner_g, k),
             device_id_type=MESH,
         ).start()
     grecv_ref[pl.ds(g, 1)] = mine.reshape(1, 8, 128)
@@ -463,18 +544,17 @@
     mine = jnp.sum(diagonal, axis=0, keepdims=True)
     px_ref[...] = mine
 
-    def one(i, _):
+    def one(m):
         pltpu.make_async_remote_copy(
             src_ref=px_ref,
             dst_ref=precv_ref.at[k],
             send_sem=send_sem.at[2, 1],
             recv_sem=recv_sem.at[2, 1],
-            device_id=(g, lax.rem(k + i, n_yz)),
+            device_id=(g, m),
             device_id_type=MESH,
         ).start()
-        return 0
-
-    lax.fori_loop(1, n_yz, one, 0)
+
+    plane(one)
     precv_ref[pl.ds(k, 1)] = mine.reshape(1, 1, 128)
     sum_copy = pltpu.make_async_remote_copy(
         src_ref=precv_ref.at[pl.ds(0, n_yz - 1)],
@@ -556,12 +636,15 @@
         small, outq, incm, incq, cmts, *tables,
     )
     vmem = pl.BlockSpec(memory_space=pltpu.VMEM)
+    hbm = pl.BlockSpec(memory_space=pltpu.HBM)
     return pl.pallas_call(
         functools.partial(kernel, n_gx, n_yz, cmts.shape[1]),
         out_shape=jax.ShapeDtypeStruct(source.shape, F32),
-        in_specs=[vmem] * len(arguments),
+        in_specs=[hbm] * len(arguments),
         out_specs=vmem,
         scratch_shapes=[
+            *[pltpu.VMEM(a.shape, a.dtype) for a in arguments],
+            pltpu.SemaphoreType.DMA((len(arguments),)),
             pltpu.VMEM((2, n_yz, 8, 128), F32),
             pltpu.VMEM((2, n_yz, 8, 128), F32),
             pltpu.VMEM((2, 4, HALO, 128), F32),
@@ -581,7 +664,7 @@
             pltpu.SemaphoreType.DMA((3, 2)),
         ],
         compiler_params=pltpu.CompilerParams(
-            collective_id=0, has_side_effects=True, vmem_limit_bytes=48 * 1024 * 1024
+            collective_id=0, has_side_effects=True, vmem_limit_bytes=63 * 1024 * 1024
         ),
     )(*arguments)
 

time: 66.7 us -> 51.5 us (0.77)
  local copies, waits for them, and re-layouts: 16.3 us -> 1.59 us
    unnamed x39 -> x1, local copies, waits for them, and re-layouts: 16.3 us -> 1.59 us
where the time goes in v2:
time: 51.5 us; the launch traced here: 51.3 us
  Pallas kernels  49.7 us (97%)
  local copies, waits for them, and re-layouts  1.59 us (3%)
    pallas_call x1, Pallas kernels, on_device(): pl.pallas_call(functools.partial(kernel, n_gx, n_yz, cmts.shape[1]), out_...  49.7 us
    unnamed x1, local copies, waits for them, and re-layouts  1.59 us

profile of v2, /device:TPU:1, one launch (start us, length us, event | category | flops | bytes accessed | tf_op | source)
XLA Modules:
  0.0 51.3 jit_solution(11074074968948849274)
XLA Ops:
  0.0 49.7 %shard_map.181 = f32[320,128]{1,0:T(8,128)} custom-call(f32[320,128]{1,0:T(8,128)} %b_hbm.1, f32[320,128]{1,0:T(8,128)} %mass_hbm.1, f32[480,128]{1,0:T(8,128)} %coef_hbm.1, f32[75,128]{1,0:T(8,128)} %flux_hbm.1, f32[320,320]{1,0:T(8,128)} %first_hbm.1, f32[320,320]{1,0:T(8,128)} %final_hbm.1, f32[320,128]{1,0:T(8,128)} %mid_hbm.1, s32[6,128]{1,0:T(8,128)} %adj_hbm.1, ...), custom_call_target="tpu_custom_call" | custom-call | tf_op jit(solution)/shard_map/pallas_call | solution.py:640
  49.7 1.6 %copy.21 = f32[320,128]{1,0:T(8,128)} copy(f32[320,128]{1,0:T(8,128)} %shard_map.181) | data formatting | bytes 327680

commit v3 on v2

--- a/solution.py
+++ b/solution.py
@@ -19,6 +19,7 @@
 CAP = 6
 FACE = 80
 HALO = 16
+HEAD = 128 - FACE
 
 
 def split_np(array):
@@ -97,11 +98,25 @@
     return jnp.dot(a, b, preferred_element_type=F32)
 
 
-def product(a_high, a_low, b):
-    b_high, b_low = split(b)
+def side_by_side(high, low):
+    return jnp.concatenate([high[:, :256], low[:, :256], high[:, 256:], low[:, 256:]], axis=1)
+
+
+def product(a, b):
+    high, low = split(b)
+    blank = jnp.zeros_like(low)
+    both = mm(
+        a,
+        jnp.concatenate(
+            [
+                jnp.concatenate([high[:256], high[:256], high[256:], high[256:]], axis=0),
+                jnp.concatenate([low[:256], blank[:256], low[256:], blank[256:]], axis=0),
+            ],
+            axis=1,
+        ),
+    )
     n = b.shape[1]
-    wide = mm(a_high, jnp.concatenate([b_high, b_low], axis=1))
-    return wide[:, :n] + wide[:, n:] + mm(a_low, b_high)
+    return both[:, :n] + both[:, n:]
 
 
 def lanes(shape):
@@ -198,6 +213,7 @@
     g, k = lax.axis_index("gx"), lax.axis_index("yz")
     wide = 8 * n_yz
     slots = CAP * n_yz
+    half = n_yz
     barrier = pltpu.get_barrier_semaphore()
 
     n_y = 8 if n_yz % 16 == 0 else n_yz // 2
@@ -222,6 +238,8 @@
         for column, dx, c in columns:
             if dx or c:
                 act(column + y * 2 + cores[c])
+
+    mine = pl.ds(pl.multiple_of(8 * k, 8), 8)
 
     def greet(device):
         pl.semaphore_signal(barrier, inc=1, device_id=(g, device), device_id_type=MESH)
@@ -265,16 +283,15 @@
     ready("mid", "final", "select", "fine", "coarse")
     first_high, first_low = split(first_ref[...])
     final_high, final_low = split(final_ref[...])
+    first = side_by_side(first_high, first_low)
+    final = side_by_side(final_high, final_low)
     select = select_ref[...]
-    pick_ref[0] = mm(select, final_high).astype(BF16)
-    pick_ref[1] = mm(select, final_low).astype(BF16)
+    pick_ref[...] = mm(select, final).astype(BF16)
 
     mid = mid_ref[...]
-    weighted = mid * product(first_high, first_low, b_ref[...])
-
-    lane = lanes((1, wide))
-    eighth = jnp.bitwise_and(lane, 7)
-    live = eighth < CAP
+    weighted = mid * product(first, b_ref[...])
+
+    lane = lanes((1, slots))
     small = small_ref[...]
     incm = incm_ref[...]
     parts = [
@@ -284,16 +301,16 @@
         incm,
         incq_ref[...],
     ]
-    target = jnp.where(live, CAP * jnp.right_shift(lane, 3) + eighth, -1)
-    spread = mm(stack_rows(parts, 16).astype(BF16), onehot(target, (slots, wide)))
+    natural = CAP * lax.rem(lane, n_yz) + lane // n_yz
+    spread = mm(stack_rows(parts, 16).astype(BF16), onehot(natural, (slots, slots)))
     spread = spread.astype(I32)
-    fine_col = jnp.where(live, 32 * spread[0:1] + spread[1:2], -1)
+    fine_col = 32 * spread[0:1] + spread[1:2]
     outq = spread[2:3]
-    owned = jnp.where(live & (spread[3:4] < hang), spread[3:4], -1)
+    owned = jnp.where(spread[3:4] < hang, spread[3:4], -1)
     incq = spread[4:5]
     cmts = cmts_ref[...]
     parts = [jnp.right_shift(cmts, 5), jnp.bitwise_and(cmts, 31)]
-    found = mm(stack_rows(parts, 16).astype(BF16), onehot(owned, (hang, wide))).astype(I32)
+    found = mm(stack_rows(parts, 16).astype(BF16), onehot(owned, (hang, slots))).astype(I32)
     coarse_col = jnp.where(owned >= 0, 32 * found[0:1] + found[1:2], -1)
     slab, side = plane_ref[0], band_ref[0]
     repeat = jnp.where(
@@ -306,9 +323,9 @@
     halo_col = jnp.full((1, 128), -1, I32)
     for i in range(4):
         halo_col = jnp.where(group == i, halo[i : i + 1] + 128 * i, halo_col)
-    oh_ref[:, 0:wide] = onehot(fine_col, (768, wide))
-    oh_ref[:, wide : 2 * wide] = onehot(coarse_col, (768, wide))
-    oh_ref[:, 2 * wide :] = onehot(halo_col, (768, 128))
+    oh_ref[:, 0:slots] = onehot(fine_col, (768, slots))
+    oh_ref[:, slots : 2 * slots] = onehot(coarse_col, (768, slots))
+    oh_ref[:, 2 * slots :] = onehot(halo_col, (768, 128))
 
     fine_w, coarse_w = fine_ref[...], coarse_ref[...]
 
@@ -332,36 +349,36 @@
         )
         tr_ref[FACE:] = jnp.concatenate([low[FACE * f : FACE * (f + 1)] for f in range(6)], axis=1)
         gathered = mm(tr_ref[...], oh_ref[...])
-        halo_out = gathered[:FACE, 2 * wide :] + gathered[FACE:, 2 * wide :]
+        halo_out = gathered[:FACE, 2 * slots :] + gathered[FACE:, 2 * slots :]
         halo_out = jnp.concatenate([halo_out, jnp.zeros((48, 128), F32)], axis=0).T
         hx_ref[step] = halo_out[0 : 4 * HALO].reshape(4, HALO, 128)
-        fine = project(fine_w, gathered[:FACE, :wide], gathered[FACE:, :wide], out_masks)
+        fine = project(fine_w, gathered[:FACE, :slots], gathered[FACE:, :slots], out_masks)
         coarse = project(
             coarse_w,
-            gathered[:FACE, wide : 2 * wide],
-            gathered[FACE:, wide : 2 * wide],
+            gathered[:FACE, slots : 2 * slots],
+            gathered[FACE:, slots : 2 * slots],
             in_masks,
         )
-        rest = coarse[48:]
-        eight = jnp.bitwise_and(lanes((32, wide)), 7)
-        tails = []
-        for i in range(4):
-            tail = jnp.where(eight == 6, pltpu.roll(rest, 6 - i, 1), 0.0)
-            if i < 2:
-                tail = jnp.where(eight == 7, pltpu.roll(rest, 3 - i, 1), tail)
-            tails.append(tail)
-        packed = jnp.where(
-            jnp.bitwise_and(lanes((128, wide)), 7) < CAP,
-            jnp.concatenate([fine, coarse[:48]], axis=0),
-            jnp.concatenate(tails, axis=0),
-        )
-        x_ref[step] = packed.T.reshape(n_yz, 8, 128)
+        rest = [coarse[HEAD:, half * c : half * c + half] for c in range(CAP)]
+        blank = jnp.zeros((32, half), F32)
+        tails = jnp.concatenate(
+            [
+                jnp.concatenate([rest[i], rest[4 + i] if i < 2 else blank], axis=1)
+                for i in range(4)
+            ],
+            axis=0,
+        )
+        packed = jnp.concatenate(
+            [jnp.concatenate([fine, coarse[:HEAD]], axis=0), tails], axis=1
+        ).T
+        for c in range(8):
+            x_ref[step, pl.ds(c, n_yz, stride=8), :] = packed[n_yz * c : n_yz * c + n_yz]
         if step == 0:
             pl.semaphore_wait(barrier, n_yz + n_gx - 2)
         def one(m):
             pltpu.make_async_remote_copy(
-                src_ref=x_ref.at[step, m],
-                dst_ref=recv_ref.at[step, k],
+                src_ref=x_ref.at[step, pl.ds(pl.multiple_of(8 * m, 8), 8)],
+                dst_ref=recv_ref.at[step, mine],
                 send_sem=send_sem.at[step, 1],
                 recv_sem=recv_sem.at[step, 1],
                 device_id=(g, m),
@@ -385,7 +402,7 @@
                 device_id=device,
                 device_id_type=MESH,
             ).start()
-        recv_ref[step, pl.ds(k, 1)] = x_ref[step, pl.ds(k, 1)]
+        recv_ref[step, mine] = x_ref[step, mine]
 
     def halo_copy(step):
         return pltpu.make_async_remote_copy(
@@ -399,8 +416,8 @@
 
     def plane_copy(step):
         return pltpu.make_async_remote_copy(
-            src_ref=x_ref.at[step, pl.ds(0, n_yz - 1)],
-            dst_ref=recv_ref.at[step, pl.ds(0, n_yz - 1)],
+            src_ref=x_ref.at[step, pl.ds(0, wide - 8)],
+            dst_ref=recv_ref.at[step, pl.ds(0, wide - 8)],
             send_sem=send_sem.at[step, 1],
             recv_sem=recv_sem.at[step, 1],
             device_id=(g, k),
@@ -410,20 +427,31 @@
     def receive(step):
         halo_copy(step).wait_recv()
         plane_copy(step).wait_recv()
-        tiles = recv_ref[step].reshape(wide, 128).T
-        eight = jnp.bitwise_and(lanes((32, wide)), 7)
-        rest = jnp.zeros((32, wide), F32)
-        for c in range(CAP):
-            i, column = c % 4, 6 + c // 4
-            moved = pltpu.roll(tiles[32 * i : 32 * i + 32], wide - (column - c), 1)
-            rest = jnp.where(eight == c, moved, rest)
+        tiles = jnp.concatenate(
+            [recv_ref[step, pl.ds(c, n_yz, stride=8), :] for c in range(8)], axis=0
+        ).T
+        rest = jnp.concatenate(
+            [
+                tiles[
+                    32 * (c % 4) : 32 * (c % 4) + 32,
+                    half * (CAP + c // 4) : half * (CAP + c // 4) + half,
+                ]
+                for c in range(CAP)
+            ],
+            axis=1,
+        )
         halo_in = hrecv_ref[step].reshape(4 * HALO, 128)
         at = jnp.right_shift(rows((4 * HALO, 128)), 4)
         drop = ((at == 0) & (g == 0)) | ((at == 1) & (g == n_gx - 1))
         halo_in = jnp.where(drop, 0.0, halo_in)
         halo_in = jnp.concatenate([halo_in, jnp.zeros((64, 128), F32)], axis=0).T[:FACE]
         values = jnp.concatenate(
-            [tiles[:FACE], jnp.concatenate([tiles[FACE:], rest], axis=0), halo_in], axis=1
+            [
+                tiles[:FACE, :slots],
+                jnp.concatenate([tiles[FACE:, :slots], rest], axis=0),
+                halo_in,
+            ],
+            axis=1,
         )
         high, low = split(values)
         near = mm(jnp.concatenate([high, low], axis=0), near_in_ref[...])
@@ -433,10 +461,10 @@
         high, low = split(u)
         node = node_ref[...]
 
-        def side_by_side(part):
+        def by_variable(part):
             return jnp.concatenate([part[64 * v : 64 * v + 64] for v in range(5)], axis=1)
 
-        high, low = side_by_side(high), side_by_side(low)
+        high, low = by_variable(high), by_variable(low)
         slopes = mm(node, jnp.concatenate([high, low, high], axis=0))
         out = []
         for a in range(5):
@@ -450,11 +478,16 @@
                         * slopes[64 * d : 64 * d + 64, 128 * v : 128 * v + 128]
                     )
             out.append(total)
-        return product(first_high, first_low, jnp.concatenate(out, axis=0))
+        return product(first, jnp.concatenate(out, axis=0))
 
     def own_near():
         near = mm(tr_ref[...], near_own_ref[...])
         return near[:FACE] + near[FACE:]
+
+    def lifted(jumps):
+        high, low = split(jumps)
+        both = mm(lift_ref[0], jnp.concatenate([high, low], axis=1))
+        return both[:, :128] + both[:, 128:] + mm(lift_ref[1], high)
 
     def finish(base, traces, near_own, near_in):
         near = near_own + near_in
@@ -466,14 +499,14 @@
             ],
             axis=0,
         )
-        return (mid * SCALE) * (base + product(lift_ref[0], lift_ref[1], jumps))
+        return (mid * SCALE) * (base + lifted(jumps))
 
     def fold(a, b):
         return jnp.sum(a * b, axis=0, keepdims=True)
 
-    traces = product(pick_ref[0], pick_ref[1], weighted)
+    traces = product(pick_ref[...], weighted)
     send(0, traces)
-    u_ref[0] = product(final_high, final_low, weighted)
+    u_ref[0] = product(final, weighted)
     nt = (((1,), (1,)), ((), ()))
     lift_ref[0] = lax.dot_general(
         first_high, select, nt, preferred_element_type=F32
@@ -483,43 +516,66 @@
     ).astype(BF16)
     ready("node", "mass", "flux", "coef", "adj")
     table = 768 + 4 * HALO
-    owned_col = jnp.broadcast_to(jnp.where(owned >= 0, owned + table, -1), (128, wide)).T
-    place = rows((wide, 128))
-    reply = jnp.where(
-        jnp.bitwise_and(place, 7) < CAP,
-        CAP * jnp.right_shift(place, 3) + jnp.bitwise_and(place, 7) + table + hang,
-        -1,
-    )
+    owned_col = jnp.broadcast_to(jnp.where(owned >= 0, owned + table, -1), (128, slots)).T
+    place = rows((slots, 128))
+    reply = CAP * lax.rem(place, n_yz) + place // n_yz + table + hang
     halo_at = rows((128, 128))
     halo_at = jnp.where(halo_at < 4 * HALO, halo_at + 768, -1)
     for f in range(6):
         adj = adj_ref[f : f + 1]
         near_own_ref[:, 128 * f : 128 * f + 128] = onehot(adj, (768, 128))
-        near_in_ref[0:wide, 128 * f : 128 * f + 128] = jnp.where(
+        near_in_ref[0:slots, 128 * f : 128 * f + 128] = jnp.where(
             owned_col == adj, 1.0, 0.0
         ).astype(BF16)
-        near_in_ref[wide : 2 * wide, 128 * f : 128 * f + 128] = jnp.where(
+        near_in_ref[slots : 2 * slots, 128 * f : 128 * f + 128] = jnp.where(
             reply == adj, 1.0, 0.0
         ).astype(BF16)
-        near_in_ref[2 * wide :, 128 * f : 128 * f + 128] = jnp.where(
+        near_in_ref[2 * slots :, 128 * f : 128 * f + 128] = jnp.where(
             halo_at == adj, 1.0, 0.0
         ).astype(BF16)
     base = volume(u_ref[0])
     near_own = own_near()
     weighted = finish(base, traces, near_own, receive(0))
 
-    traces = product(pick_ref[0], pick_ref[1], weighted)
+    traces = product(pick_ref[...], weighted)
     send(1, traces)
-    u_ref[1] = product(final_high, final_low, weighted)
+    u_ref[1] = product(final, weighted)
     base = volume(u_ref[1])
     near_own = own_near()
     r, u1 = u_ref[0], u_ref[1]
     g00, g01, g11 = fold(r, r), fold(r, u1), fold(u1, u1)
     weighted = finish(base, traces, near_own, receive(1))
-    u2 = product(final_high, final_low, weighted)
-
-    mine = stack_rows([g00, g01, g11, fold(r, u2), fold(u1, u2), fold(u2, u2)], 8)
-    gx_ref[...] = mine
+    u2 = product(final, weighted)
+
+    gram = stack_rows([g00, g01, g11, fold(r, u2), fold(u1, u2), fold(u2, u2)], 8)
+    column = jnp.sum(gram, axis=1, keepdims=True)
+    gram = jnp.where(rows((8, 128)) == lanes((8, 128)), column, 0.0)
+    gram = jnp.sum(gram, axis=0, keepdims=True)
+    px_ref[...] = gram
+
+    def one(m):
+        pltpu.make_async_remote_copy(
+            src_ref=px_ref,
+            dst_ref=precv_ref.at[k],
+            send_sem=send_sem.at[2, 1],
+            recv_sem=recv_sem.at[2, 1],
+            device_id=(g, m),
+            device_id_type=MESH,
+        ).start()
+
+    plane(one)
+    precv_ref[pl.ds(k, 1)] = gram.reshape(1, 1, 128)
+    sum_copy = pltpu.make_async_remote_copy(
+        src_ref=precv_ref.at[pl.ds(0, n_yz - 1)],
+        dst_ref=precv_ref.at[pl.ds(0, n_yz - 1)],
+        send_sem=send_sem.at[2, 1],
+        recv_sem=recv_sem.at[2, 1],
+        device_id=(g, k),
+        device_id_type=MESH,
+    )
+    sum_copy.wait_recv()
+    gram = jnp.sum(precv_ref[...], axis=0)
+    gx_ref[...] = gram
     for partner_g in gx_partners:
         pltpu.make_async_remote_copy(
             src_ref=gx_ref,
@@ -529,7 +585,7 @@
             device_id=(partner_g, k),
             device_id_type=MESH,
         ).start()
-    grecv_ref[pl.ds(g, 1)] = mine.reshape(1, 8, 128)
+    grecv_ref[pl.ds(g, 1)] = gram.reshape(1, 1, 128)
     gram_copy = pltpu.make_async_remote_copy(
         src_ref=grecv_ref.at[pl.ds(0, n_gx - 1)],
         dst_ref=grecv_ref.at[pl.ds(0, n_gx - 1)],
@@ -539,33 +595,7 @@
         device_id_type=MESH,
     )
     gram_copy.wait_recv()
-    column = jnp.sum(jnp.sum(grecv_ref[...], axis=0), axis=1, keepdims=True)
-    diagonal = jnp.where(rows((8, 128)) == lanes((8, 128)), column, 0.0)
-    mine = jnp.sum(diagonal, axis=0, keepdims=True)
-    px_ref[...] = mine
-
-    def one(m):
-        pltpu.make_async_remote_copy(
-            src_ref=px_ref,
-            dst_ref=precv_ref.at[k],
-            send_sem=send_sem.at[2, 1],
-            recv_sem=recv_sem.at[2, 1],
-            device_id=(g, m),
-            device_id_type=MESH,
-        ).start()
-
-    plane(one)
-    precv_ref[pl.ds(k, 1)] = mine.reshape(1, 1, 128)
-    sum_copy = pltpu.make_async_remote_copy(
-        src_ref=precv_ref.at[pl.ds(0, n_yz - 1)],
-        dst_ref=precv_ref.at[pl.ds(0, n_yz - 1)],
-        send_sem=send_sem.at[2, 1],
-        recv_sem=recv_sem.at[2, 1],
-        device_id=(g, k),
-        device_id_type=MESH,
-    )
-    sum_copy.wait_recv()
-    total = jnp.sum(precv_ref[...], axis=0)
+    total = jnp.sum(grecv_ref[...], axis=0)
     at = lanes((1, 128))
 
     def entry(i):
@@ -630,7 +660,7 @@
 ):
     del proprietor
     tables = [jnp.asarray(t) for t in gll_tables()]
-    wide = 8 * n_yz
+    wide, slots = 8 * n_yz, CAP * n_yz
     arguments = (
         source, mass, coupling, flux, first, final, middle, adjacent, plane, band,
         small, outq, incm, incq, cmts, *tables,
@@ -645,18 +675,18 @@
         scratch_shapes=[
             *[pltpu.VMEM(a.shape, a.dtype) for a in arguments],
             pltpu.SemaphoreType.DMA((len(arguments),)),
-            pltpu.VMEM((2, n_yz, 8, 128), F32),
-            pltpu.VMEM((2, n_yz, 8, 128), F32),
+            pltpu.VMEM((2, wide, 128), F32),
+            pltpu.VMEM((2, wide, 128), F32),
             pltpu.VMEM((2, 4, HALO, 128), F32),
             pltpu.VMEM((2, 4, HALO, 128), F32),
-            pltpu.VMEM((8, 128), F32),
-            pltpu.VMEM((n_gx, 8, 128), F32),
+            pltpu.VMEM((1, 128), F32),
+            pltpu.VMEM((n_gx, 1, 128), F32),
             pltpu.VMEM((1, 128), F32),
             pltpu.VMEM((n_yz, 1, 128), F32),
-            pltpu.VMEM((768, 2 * wide + 128), BF16),
+            pltpu.VMEM((768, 2 * slots + 128), BF16),
             pltpu.VMEM((768, 768), BF16),
-            pltpu.VMEM((2 * wide + 128, 768), BF16),
-            pltpu.VMEM((2, 480, 320), BF16),
+            pltpu.VMEM((2 * slots + 128, 768), BF16),
+            pltpu.VMEM((480, 640), BF16),
             pltpu.VMEM((2, 320, 480), BF16),
             pltpu.VMEM((2 * FACE, 768), BF16),
             pltpu.VMEM((2, 320, 128), F32),

time: 51.5 us -> 50 us (0.971)
  Pallas kernels: 49.7 us -> 48.2 us
    pallas_call x1, Pallas kernels: 49.7 us -> 48.2 us  [on_device(): pl.pallas_call(functools.partial(kernel, n_gx, n_yz, cmts.shape[1]), out_...]
where the time goes in v3:
time: 50 us; the launch traced here: 49.8 us
  Pallas kernels  48.2 us (96%)
  local copies, waits for them, and re-layouts  1.59 us (3%)
    pallas_call x1, Pallas kernels, on_device(): pl.pallas_call(functools.partial(kernel, n_gx, n_yz, cmts.shape[1]), out_...  48.2 us
    unnamed x1, local copies, waits for them, and re-layouts  1.59 us

profile of v3, /device:TPU:1, one launch (start us, length us, event | category | flops | bytes accessed | tf_op | source)
XLA Modules:
  0.0 49.8 jit_solution(4056610087215262688)
XLA Ops:
  0.0 48.2 %shard_map.181 = f32[320,128]{1,0:T(8,128)} custom-call(f32[320,128]{1,0:T(8,128)} %b_hbm.1, f32[320,128]{1,0:T(8,128)} %mass_hbm.1, f32[480,128]{1,0:T(8,128)} %coef_hbm.1, f32[75,128]{1,0:T(8,128)} %flux_hbm.1, f32[320,320]{1,0:T(8,128)} %first_hbm.1, f32[320,320]{1,0:T(8,128)} %final_hbm.1, f32[320,128]{1,0:T(8,128)} %mid_hbm.1, s32[6,128]{1,0:T(8,128)} %adj_hbm.1, ...), custom_call_target="tpu_custom_call" | custom-call | tf_op jit(solution)/shard_map/pallas_call | solution.py:670
  48.2 1.6 %copy.21 = f32[320,128]{1,0:T(8,128)} copy(f32[320,128]{1,0:T(8,128)} %shard_map.181) | data formatting | bytes 327680

commit v4 on v3

--- a/solution.py
+++ b/solution.py
@@ -213,7 +213,6 @@
     g, k = lax.axis_index("gx"), lax.axis_index("yz")
     wide = 8 * n_yz
     slots = CAP * n_yz
-    half = n_yz
     barrier = pltpu.get_barrier_semaphore()
 
     n_y = 8 if n_yz % 16 == 0 else n_yz // 2
@@ -227,21 +226,22 @@
     ]
     cores = (core, 1 - core)
 
-    def plane(act):
+    def plane(act, start=0, end=n_y):
         def one(i, _):
             at = lax.rem(y + outward(i, n_y), n_y) * 2
-            for column, _, c in columns:
-                act(column + at + cores[c])
+            for r, (column, _, c) in enumerate(columns):
+                act(column + at + cores[c], i * 2 * n_x + r)
             return 0
 
-        lax.fori_loop(0, n_y - 1, one, 0)
-        for column, dx, c in columns:
-            if dx or c:
-                act(column + y * 2 + cores[c])
+        lax.fori_loop(start, min(end, n_y - 1), one, 0)
+        if end == n_y:
+            for r, (column, dx, c) in enumerate(columns):
+                if dx or c:
+                    act(column + y * 2 + cores[c], (n_y - 1) * 2 * n_x + r)
 
     mine = pl.ds(pl.multiple_of(8 * k, 8), 8)
 
-    def greet(device):
+    def greet(device, _):
         pl.semaphore_signal(barrier, inc=1, device_id=(g, device), device_id_type=MESH)
 
     plane(greet)
@@ -279,6 +279,20 @@
         for name in wanted:
             loads[name].wait()
 
+    half = n_yz // 2
+    part = 8 * half
+    place = lanes((1, 2 * part))
+    place_c = lax.rem(place, part) // half
+    place_i = (place // part) * half + lax.rem(place, half)
+    jx = lax.rem(place_i, 2 * n_x) // 2
+    place_x = jnp.zeros_like(jx)
+    for j, dx in enumerate(far_first(n_x)):
+        place_x = jnp.where(jx == j, dx, place_x)
+    place_x = lax.rem(x + place_x, n_x)
+    place_y = lax.rem(y + outward(place_i // (2 * n_x), n_y), n_y)
+    place_core = lax.rem(core + 1 + place_i, 2)
+    place_device = (place_x * n_y + place_y) * 2 + place_core
+
     ready("first", "b", "small", "outq", "incm", "incq", "cmts", "plane", "band")
     ready("mid", "final", "select", "fine", "coarse")
     first_high, first_low = split(first_ref[...])
@@ -291,7 +305,6 @@
     mid = mid_ref[...]
     weighted = mid * product(first, b_ref[...])
 
-    lane = lanes((1, slots))
     small = small_ref[...]
     incm = incm_ref[...]
     parts = [
@@ -301,17 +314,18 @@
         incm,
         incq_ref[...],
     ]
-    natural = CAP * lax.rem(lane, n_yz) + lane // n_yz
-    spread = mm(stack_rows(parts, 16).astype(BF16), onehot(natural, (slots, slots)))
+    live = place_c < CAP
+    target = jnp.where(live, CAP * place_device + place_c, -1)
+    spread = mm(stack_rows(parts, 16).astype(BF16), onehot(target, (slots, 2 * part)))
     spread = spread.astype(I32)
-    fine_col = 32 * spread[0:1] + spread[1:2]
+    fine_col = jnp.where(live, 32 * spread[0:1] + spread[1:2], -1)
     outq = spread[2:3]
-    owned = jnp.where(spread[3:4] < hang, spread[3:4], -1)
+    asked = jnp.where(live & (spread[3:4] < hang), spread[3:4], -1)
     incq = spread[4:5]
     cmts = cmts_ref[...]
     parts = [jnp.right_shift(cmts, 5), jnp.bitwise_and(cmts, 31)]
-    found = mm(stack_rows(parts, 16).astype(BF16), onehot(owned, (hang, slots))).astype(I32)
-    coarse_col = jnp.where(owned >= 0, 32 * found[0:1] + found[1:2], -1)
+    found = mm(stack_rows(parts, 16).astype(BF16), onehot(asked, (hang, 2 * part))).astype(I32)
+    coarse_col = jnp.where(asked >= 0, 32 * found[0:1] + found[1:2], -1)
     slab, side = plane_ref[0], band_ref[0]
     repeat = jnp.where(
         jnp.bitwise_and(lanes((HALO, 128)), HALO - 1) == rows((HALO, 128)), 1.0, 0.0
@@ -323,9 +337,12 @@
     halo_col = jnp.full((1, 128), -1, I32)
     for i in range(4):
         halo_col = jnp.where(group == i, halo[i : i + 1] + 128 * i, halo_col)
-    oh_ref[:, 0:slots] = onehot(fine_col, (768, slots))
-    oh_ref[:, slots : 2 * slots] = onehot(coarse_col, (768, slots))
-    oh_ref[:, 2 * slots :] = onehot(halo_col, (768, 128))
+    for i in range(2):
+        cut = slice(part * i, part * i + part)
+        at = 2 * part * i
+        oh_ref[:, at : at + part] = onehot(fine_col[:, cut], (768, part))
+        oh_ref[:, at + part : at + 2 * part] = onehot(coarse_col[:, cut], (768, part))
+    oh_ref[:, 4 * part :] = onehot(halo_col, (768, 128))
 
     fine_w, coarse_w = fine_ref[...], coarse_ref[...]
 
@@ -335,49 +352,42 @@
     out_masks, in_masks = masks(outq), masks(incq)
 
     def project(matrix, high, low, mask):
-        def spread_out(part):
-            part = part.astype(BF16)
-            return jnp.concatenate([part * mask[q] for q in range(4)], axis=0)
+        def spread_out(values):
+            values = values.astype(BF16)
+            return jnp.concatenate([values * mask[q] for q in range(4)], axis=0)
 
         both = mm(matrix, spread_out(high))
         return both[:FACE] + both[FACE:] + mm(matrix[:FACE], spread_out(low))
 
-    def send(step, u_traces):
-        high, low = split(u_traces)
-        tr_ref[0:FACE] = jnp.concatenate(
-            [high[FACE * f : FACE * (f + 1)] for f in range(6)], axis=1
-        )
-        tr_ref[FACE:] = jnp.concatenate([low[FACE * f : FACE * (f + 1)] for f in range(6)], axis=1)
-        gathered = mm(tr_ref[...], oh_ref[...])
-        halo_out = gathered[:FACE, 2 * slots :] + gathered[FACE:, 2 * slots :]
-        halo_out = jnp.concatenate([halo_out, jnp.zeros((48, 128), F32)], axis=0).T
-        hx_ref[step] = halo_out[0 : 4 * HALO].reshape(4, HALO, 128)
-        fine = project(fine_w, gathered[:FACE, :slots], gathered[FACE:, :slots], out_masks)
+    def send_part(step, i):
+        cut = slice(part * i, part * i + part)
+        gathered = mm(tr_ref[...], oh_ref[:, 2 * part * i : 2 * part * i + 2 * part])
+        fine = project(
+            fine_w, gathered[:FACE, :part], gathered[FACE:, :part], [m[:, cut] for m in out_masks]
+        )
         coarse = project(
-            coarse_w,
-            gathered[:FACE, slots : 2 * slots],
-            gathered[FACE:, slots : 2 * slots],
-            in_masks,
+            coarse_w, gathered[:FACE, part:], gathered[FACE:, part:], [m[:, cut] for m in in_masks]
         )
         rest = [coarse[HEAD:, half * c : half * c + half] for c in range(CAP)]
         blank = jnp.zeros((32, half), F32)
         tails = jnp.concatenate(
             [
-                jnp.concatenate([rest[i], rest[4 + i] if i < 2 else blank], axis=1)
-                for i in range(4)
+                jnp.concatenate([rest[j], rest[4 + j] if j < 2 else blank], axis=1)
+                for j in range(4)
             ],
             axis=0,
         )
-        packed = jnp.concatenate(
-            [jnp.concatenate([fine, coarse[:HEAD]], axis=0), tails], axis=1
-        ).T
+        head = jnp.concatenate([fine[:, : CAP * half], coarse[:HEAD, : CAP * half]], axis=0)
+        packed = jnp.concatenate([head, tails], axis=1).T
         for c in range(8):
-            x_ref[step, pl.ds(c, n_yz, stride=8), :] = packed[n_yz * c : n_yz * c + n_yz]
-        if step == 0:
-            pl.semaphore_wait(barrier, n_yz + n_gx - 2)
-        def one(m):
+            x_ref[step, i, pl.ds(c, half, stride=8), :] = packed[
+                half * c : half * c + half
+            ]
+
+    def start_part(step, i, start, end):
+        def one(m, at):
             pltpu.make_async_remote_copy(
-                src_ref=x_ref.at[step, pl.ds(pl.multiple_of(8 * m, 8), 8)],
+                src_ref=x_ref.at[step, i, pl.ds(pl.multiple_of(8 * at - part * i, 8), 8)],
                 dst_ref=recv_ref.at[step, mine],
                 send_sem=send_sem.at[step, 1],
                 recv_sem=recv_sem.at[step, 1],
@@ -385,7 +395,24 @@
                 device_id_type=MESH,
             ).start()
 
-        plane(one)
+        plane(one, start, end)
+
+    def send(step, u_traces):
+        high, low = split(u_traces)
+        tr_ref[0:FACE] = jnp.concatenate(
+            [high[FACE * f : FACE * (f + 1)] for f in range(6)], axis=1
+        )
+        tr_ref[FACE:] = jnp.concatenate([low[FACE * f : FACE * (f + 1)] for f in range(6)], axis=1)
+        send_part(step, 0)
+        if step == 0:
+            pl.semaphore_wait(barrier, n_yz + n_gx - 2)
+        start_part(step, 0, 0, n_y // 2)
+        send_part(step, 1)
+        start_part(step, 1, n_y // 2, n_y)
+        halo_out = mm(tr_ref[...], oh_ref[:, 4 * part :])
+        halo_out = halo_out[:FACE] + halo_out[FACE:]
+        halo_out = jnp.concatenate([halo_out, jnp.zeros((48, 128), F32)], axis=0).T
+        hx_ref[step] = halo_out[0 : 4 * HALO].reshape(4, HALO, 128)
         up_g, down_g = lax.rem(g + 1, n_gx), lax.rem(g + n_gx - 1, n_gx)
         up_k, down_k = lax.rem(k + 1, n_yz), lax.rem(k + n_yz - 1, n_yz)
         for source, target, device in (
@@ -402,7 +429,7 @@
                 device_id=device,
                 device_id_type=MESH,
             ).start()
-        recv_ref[step, mine] = x_ref[step, mine]
+        recv_ref[step, mine] = x_ref[step, 1, pl.ds(part - 8, 8)]
 
     def halo_copy(step):
         return pltpu.make_async_remote_copy(
@@ -416,7 +443,7 @@
 
     def plane_copy(step):
         return pltpu.make_async_remote_copy(
-            src_ref=x_ref.at[step, pl.ds(0, wide - 8)],
+            src_ref=recv_ref.at[step, pl.ds(0, wide - 8)],
             dst_ref=recv_ref.at[step, pl.ds(0, wide - 8)],
             send_sem=send_sem.at[step, 1],
             recv_sem=recv_sem.at[step, 1],
@@ -434,7 +461,7 @@
             [
                 tiles[
                     32 * (c % 4) : 32 * (c % 4) + 32,
-                    half * (CAP + c // 4) : half * (CAP + c // 4) + half,
+                    n_yz * (CAP + c // 4) : n_yz * (CAP + c // 4) + n_yz,
                 ]
                 for c in range(CAP)
             ],
@@ -516,9 +543,14 @@
     ).astype(BF16)
     ready("node", "mass", "flux", "coef", "adj")
     table = 768 + 4 * HALO
-    owned_col = jnp.broadcast_to(jnp.where(owned >= 0, owned + table, -1), (128, slots)).T
-    place = rows((slots, 128))
-    reply = CAP * lax.rem(place, n_yz) + place // n_yz + table + hang
+    lane = lanes((1, slots))
+    natural = CAP * lax.rem(lane, n_yz) + lane // n_yz
+    owned = mm(stack_rows([incm], 16).astype(BF16), onehot(natural, (slots, slots)))[0:1]
+    owned = owned.astype(I32)
+    owned = jnp.where(owned < hang, owned + table, -1)
+    owned_col = jnp.broadcast_to(owned, (128, slots)).T
+    slot = rows((slots, 128))
+    reply = CAP * lax.rem(slot, n_yz) + slot // n_yz + table + hang
     halo_at = rows((128, 128))
     halo_at = jnp.where(halo_at < 4 * HALO, halo_at + 768, -1)
     for f in range(6):
@@ -553,7 +585,7 @@
     gram = jnp.sum(gram, axis=0, keepdims=True)
     px_ref[...] = gram
 
-    def one(m):
+    def one(m, _):
         pltpu.make_async_remote_copy(
             src_ref=px_ref,
             dst_ref=precv_ref.at[k],
@@ -675,7 +707,7 @@
         scratch_shapes=[
             *[pltpu.VMEM(a.shape, a.dtype) for a in arguments],
             pltpu.SemaphoreType.DMA((len(arguments),)),
-            pltpu.VMEM((2, wide, 128), F32),
+            pltpu.VMEM((2, 2, wide // 2, 128), F32),
             pltpu.VMEM((2, wide, 128), F32),
             pltpu.VMEM((2, 4, HALO, 128), F32),
             pltpu.VMEM((2, 4, HALO, 128), F32),
@@ -683,7 +715,7 @@
             pltpu.VMEM((n_gx, 1, 128), F32),
             pltpu.VMEM((1, 128), F32),
             pltpu.VMEM((n_yz, 1, 128), F32),
-            pltpu.VMEM((768, 2 * slots + 128), BF16),
+            pltpu.VMEM((768, 4 * wide // 2 + 128), BF16),
             pltpu.VMEM((768, 768), BF16),
             pltpu.VMEM((2 * slots + 128, 768), BF16),
             pltpu.VMEM((480, 640), BF16),

time: 50 us -> 49.8 us (level)
  no operation moved by 1% of the time
where the time goes in v4:
time: 49.8 us; the launch traced here: 49.7 us
  Pallas kernels  48.1 us (97%)
  local copies, waits for them, and re-layouts  1.59 us (3%)
    pallas_call x1, Pallas kernels, on_device(): pl.pallas_call(functools.partial(kernel, n_gx, n_yz, cmts.shape[1]), out_...  48.1 us
    unnamed x1, local copies, waits for them, and re-layouts  1.59 us

profile of v4, /device:TPU:1, one launch (start us, length us, event | category | flops | bytes accessed | tf_op | source)
XLA Modules:
  0.0 49.7 jit_solution(13053635716445945879)
XLA Ops:
  0.0 48.1 %shard_map.181 = f32[320,128]{1,0:T(8,128)} custom-call(f32[320,128]{1,0:T(8,128)} %b_hbm.1, f32[320,128]{1,0:T(8,128)} %mass_hbm.1, f32[480,128]{1,0:T(8,128)} %coef_hbm.1, f32[75,128]{1,0:T(8,128)} %flux_hbm.1, f32[320,320]{1,0:T(8,128)} %first_hbm.1, f32[320,320]{1,0:T(8,128)} %final_hbm.1, f32[320,128]{1,0:T(8,128)} %mid_hbm.1, s32[6,128]{1,0:T(8,128)} %adj_hbm.1, ...), custom_call_target="tpu_custom_call" | custom-call | tf_op jit(solution)/shard_map/pallas_call | solution.py:702
  48.1 1.6 %copy.21 = f32[320,128]{1,0:T(8,128)} copy(f32[320,128]{1,0:T(8,128)} %shard_map.181) | data formatting | bytes 327680

commit v5 on v4

--- a/solution.py
+++ b/solution.py
@@ -219,25 +219,23 @@
     n_x = n_yz // (2 * n_y)
     x, y, core = k // (2 * n_y), lax.rem(k // 2, n_y), lax.rem(k, 2)
 
-    columns = [
-        (lax.rem(x + dx, n_x) * n_y * 2, dx, c)
-        for dx in far_first(n_x)
-        for c in (1, 0)
-    ]
-    cores = (core, 1 - core)
+    heights = [lax.rem(y + dy, n_y) * 2 for dy in far_first(n_y)]
+    cores = (1 - core, core)
 
     def plane(act, start=0, end=n_y):
+        def row(column, i, last):
+            for j in range(start, end):
+                for c in range(2):
+                    if not (last and j == n_y - 1 and c == 1):
+                        act(column + heights[j] + cores[c], (j * n_x + i) * 2 + c)
+
         def one(i, _):
-            at = lax.rem(y + outward(i, n_y), n_y) * 2
-            for r, (column, _, c) in enumerate(columns):
-                act(column + at + cores[c], i * 2 * n_x + r)
+            row(lax.rem(x + outward(i, n_x), n_x) * n_y * 2, i, False)
             return 0
 
-        lax.fori_loop(start, min(end, n_y - 1), one, 0)
-        if end == n_y:
-            for r, (column, dx, c) in enumerate(columns):
-                if dx or c:
-                    act(column + y * 2 + cores[c], (n_y - 1) * 2 * n_x + r)
+        if n_x > 1:
+            lax.fori_loop(0, n_x - 1, one, 0)
+        row(x * n_y * 2, n_x - 1, True)
 
     mine = pl.ds(pl.multiple_of(8 * k, 8), 8)
 

time: 49.8 us -> 49.4 us (level)
  Pallas kernels: 48.1 us -> 47.6 us
where the time goes in v5:
time: 49.4 us; the launch traced here: 49.3 us
  Pallas kernels  47.6 us (96%)
  local copies, waits for them, and re-layouts  1.59 us (3%)
    pallas_call x1, Pallas kernels, on_device(): pl.pallas_call(functools.partial(kernel, n_gx, n_yz, cmts.shape[1]), out_...  47.6 us
    unnamed x1, local copies, waits for them, and re-layouts  1.59 us

profile of v5, /device:TPU:1, one launch (start us, length us, event | category | flops | bytes accessed | tf_op | source)
XLA Modules:
  0.0 49.3 jit_solution(8883550329514597168)
XLA Ops:
  0.0 47.6 %shard_map.181 = f32[320,128]{1,0:T(8,128)} custom-call(f32[320,128]{1,0:T(8,128)} %b_hbm.1, f32[320,128]{1,0:T(8,128)} %mass_hbm.1, f32[480,128]{1,0:T(8,128)} %coef_hbm.1, f32[75,128]{1,0:T(8,128)} %flux_hbm.1, f32[320,320]{1,0:T(8,128)} %first_hbm.1, f32[320,320]{1,0:T(8,128)} %final_hbm.1, f32[320,128]{1,0:T(8,128)} %mid_hbm.1, s32[6,128]{1,0:T(8,128)} %adj_hbm.1, ...), custom_call_target="tpu_custom_call" | custom-call | tf_op jit(solution)/shard_map/pallas_call | solution.py:700
  47.7 1.6 %copy.21 = f32[320,128]{1,0:T(8,128)} copy(f32[320,128]{1,0:T(8,128)} %shard_map.181) | data formatting | bytes 327680

commit v6 on v5

--- a/solution.py
+++ b/solution.py
@@ -171,6 +171,7 @@
     fine_hbm,
     coarse_hbm,
     select_hbm,
+    out_hbm,
     out_ref,
     b_ref,
     mass_ref,
@@ -209,6 +210,7 @@
     u_ref,
     send_sem,
     recv_sem,
+    store_sem,
 ):
     g, k = lax.axis_index("gx"), lax.axis_index("yz")
     wide = 8 * n_yz
@@ -632,13 +634,20 @@
         return jnp.sum(jnp.where(at == i, total, 0.0), axis=1, keepdims=True)
 
     c_r, c_u = coefficients(*[entry(i) for i in range(6)])
-    out_ref[...] = c_r * u_ref[0] + c_u * u_ref[1]
+    stores = []
+    for i in range(2):
+        at = pl.ds(160 * i, 160)
+        out_ref[at] = c_r * u_ref[0, at] + c_u * u_ref[1, at]
+        stores.append(pltpu.make_async_copy(out_ref.at[at], out_hbm.at[at], store_sem.at[i]))
+        stores[i].start()
 
     for step in range(2):
         halo_copy(step).wait_send()
         plane_copy(step).wait_send()
     gram_copy.wait_send()
     sum_copy.wait_send()
+    for store in stores:
+        store.wait()
 
 
 def coefficients(g00, g01, g11, g02, g12, g22):
@@ -695,14 +704,14 @@
         source, mass, coupling, flux, first, final, middle, adjacent, plane, band,
         small, outq, incm, incq, cmts, *tables,
     )
-    vmem = pl.BlockSpec(memory_space=pltpu.VMEM)
     hbm = pl.BlockSpec(memory_space=pltpu.HBM)
     return pl.pallas_call(
         functools.partial(kernel, n_gx, n_yz, cmts.shape[1]),
         out_shape=jax.ShapeDtypeStruct(source.shape, F32),
         in_specs=[hbm] * len(arguments),
-        out_specs=vmem,
+        out_specs=hbm,
         scratch_shapes=[
+            pltpu.VMEM(source.shape, F32),
             *[pltpu.VMEM(a.shape, a.dtype) for a in arguments],
             pltpu.SemaphoreType.DMA((len(arguments),)),
             pltpu.VMEM((2, 2, wide // 2, 128), F32),
@@ -722,6 +731,7 @@
             pltpu.VMEM((2, 320, 128), F32),
             pltpu.SemaphoreType.DMA((3, 2)),
             pltpu.SemaphoreType.DMA((3, 2)),
+            pltpu.SemaphoreType.DMA((2,)),
         ],
         compiler_params=pltpu.CompilerParams(
             collective_id=0, has_side_effects=True, vmem_limit_bytes=63 * 1024 * 1024

time: 49.4 us -> 49.4 us (level)
  no operation moved by 1% of the time
where the time goes in v6:
time: 49.4 us; the launch traced here: 49.2 us
  Pallas kernels  47.6 us (96%)
  local copies, waits for them, and re-layouts  1.59 us (3%)
    pallas_call x1, Pallas kernels, on_device(): pl.pallas_call(functools.partial(kernel, n_gx, n_yz, cmts.shape[1]), out_...  47.6 us
    unnamed x1, local copies, waits for them, and re-layouts  1.59 us

profile of v6, /device:TPU:1, one launch (start us, length us, event | category | flops | bytes accessed | tf_op | source)
XLA Modules:
  0.0 49.2 jit_solution(15124914655213809086)
XLA Ops:
  0.0 47.6 %shard_map.181 = f32[320,128]{1,0:T(8,128)} custom-call(f32[320,128]{1,0:T(8,128)} %b_hbm.1, f32[320,128]{1,0:T(8,128)} %mass_hbm.1, f32[480,128]{1,0:T(8,128)} %coef_hbm.1, f32[75,128]{1,0:T(8,128)} %flux_hbm.1, f32[320,320]{1,0:T(8,128)} %first_hbm.1, f32[320,320]{1,0:T(8,128)} %final_hbm.1, f32[320,128]{1,0:T(8,128)} %mid_hbm.1, s32[6,128]{1,0:T(8,128)} %adj_hbm.1, ...), custom_call_target="tpu_custom_call" | custom-call | tf_op jit(solution)/shard_map/pallas_call | solution.py:708
  47.7 1.6 %copy.21 = f32[320,128]{1,0:T(8,128)} copy(f32[320,128]{1,0:T(8,128)} %shard_map.181) | data formatting | bytes 327680
